TPU v7x, 256 devices: a whole 4x4x8 slice. The times are simulated.
256 devices in a mesh: tok: 16 (over z, core), voc: 16 (over x, y).
Axes of the slice: x: 4, y: 4, z: 8, core: 2. Of those that a mesh axis runs over, the one named last changes fastest.
Arguments:
- target_logits: bfloat16 [2048, 128256], P('tok', 'voc'), may hold values from -30 to 250
- hidden: bfloat16 [2048, 4096], P('tok', 'voc'), may hold values from -4 to 4
- gain: bfloat16 [4096], P('voc'), may hold values from 0.099609375 to 1.8984375
- head_weight: bfloat16 [4096, 16000], P(None, 'voc'), may hold values from -5 to 5
- draft_ids: int32 [16000], replicated, may hold values from 0 to 128255, as said below
- token_ids: int32 [2048], P('tok'), may hold values from 0 to 128255, as said below
Outputs:
- d_hidden: float32 [2048, 4096], P('tok', 'voc')
- token_loss: float32 [2048], P('tok')
Inputs may be any that keep to these rules, and one draw needn't show every extreme that they name: `draft_ids`: the 16000 ids are distinct. Entry i belongs to voc index i // 1000. Of the 1000 ids of one voc index at most 152 lie in one block of 8016 consecutive ids, and for every voc index some block holds exactly 152 of them. `token_ids`: the first token of each block of 128 tokens is one of draft_ids.
All inputs are finite; a program needn't handle non-finite values.
Results may differ from a plain program's by a relative error of at most 0.0058.
Values may be sent and summed in bfloat16 or wider, within the bound.
A program may use at most 64 MiB of HBM per device.

v0:
```python
import jax
import jax.numpy as jnp
from jax import lax
from jax.sharding import PartitionSpec as P

epsilon = 1e-05


def joined(value, axis, join):
    pieces = jax.tree.map(lambda part: lax.all_gather(part, axis), value)
    head = jax.tree.map(lambda part: part[0], pieces)
    tail = jax.tree.map(lambda part: part[1:], pieces)
    total, _ = lax.scan(lambda total, share: (join(total, share), None), head, tail)
    return total


def pair_merge(earlier, later):
    top_value = jnp.maximum(earlier[0], later[0])
    total_sum = earlier[1] * jnp.exp(earlier[0] - top_value) + later[1] * jnp.exp(
        later[0] - top_value
    )
    return (top_value, total_sum)


def joined_merge(earlier, later):
    target_top, target_total = pair_merge((earlier[0], earlier[1]), (later[0], later[1]))
    picked_top = jnp.maximum(earlier[2], later[2])
    left_factor = jnp.exp(earlier[2] - picked_top)
    right_factor = jnp.exp(later[2] - picked_top)
    picked_total = earlier[3] * left_factor + later[3] * right_factor
    picked_cross = earlier[4] * left_factor + later[4] * right_factor
    draft_top, draft_total = pair_merge((earlier[5], earlier[6]), (later[5], later[6]))
    return (
        target_top,
        target_total,
        picked_top,
        picked_total,
        picked_cross,
        draft_top,
        draft_total,
    )


def per_device(target_logits, hidden, gain, head_weight, draft_ids, token_ids):
    tok_rows = hidden.shape[0]
    part_width = hidden.shape[1]
    shards = lax.axis_size("voc")
    shard_id = lax.axis_index("voc")
    vocab_dev = target_logits.shape[1]
    draft_dev = head_weight.shape[1]
    slot_count = 8 * (5 * draft_dev // (16 * shards))
    total_tokens = tok_rows * lax.axis_size("tok")
    inside = jnp.any(token_ids[:, None] == draft_ids[None, :], axis=1).astype(jnp.float32)
    valid_total = lax.psum(jnp.sum(inside), "tok")
    weight = inside * (total_tokens / valid_total)
    logits_wide = target_logits.astype(jnp.float32)
    top_target = jnp.max(logits_wide, axis=1)
    total_target = jnp.sum(jnp.exp(logits_wide - top_target[:, None]), axis=1)
    owners = draft_ids.reshape(shards, draft_dev)
    home_shard = owners // vocab_dev
    shard_range = jnp.arange(shards, dtype=jnp.int32)
    hit_table = (home_shard[:, :, None] == shard_range[None, None, :]).astype(jnp.bfloat16)
    entry_range = jnp.arange(draft_dev, dtype=jnp.int32)
    lower_ones = (entry_range[None, :] < entry_range[:, None]).astype(jnp.bfloat16)
    earlier_hits = jnp.einsum(
        "ij,sjk->sik", lower_ones, hit_table, preferred_element_type=jnp.float32
    )
    rank_before = jnp.sum(earlier_hits * hit_table.astype(jnp.float32), axis=2).astype(jnp.int32)
    is_mine = home_shard == shard_id
    local_column = owners - shard_id * vocab_dev
    slot_range = jnp.arange(slot_count, dtype=jnp.int32)
    slot_match = is_mine[:, :, None] & (rank_before[:, :, None] == slot_range[None, None, :])
    slot_column = jnp.sum(jnp.where(slot_match, local_column[:, :, None] + 1, 0), axis=1) - 1

    def pick_block(columns):
        one_hot = (jnp.arange(vocab_dev, dtype=jnp.int32)[:, None] == columns[None, :]).astype(
            jnp.bfloat16
        )
        return jnp.dot(target_logits, one_hot, preferred_element_type=jnp.float32).astype(
            jnp.bfloat16
        )

    outgoing = lax.map(pick_block, slot_column)
    incoming = lax.all_to_all(outgoing, "voc", split_axis=0, concat_axis=0, tiled=True)
    my_home = lax.dynamic_index_in_dim(home_shard, shard_id, 0, keepdims=False)
    my_rank = lax.dynamic_index_in_dim(rank_before, shard_id, 0, keepdims=False)
    select_home = my_home[None, :] == shard_range[:, None]
    select_rank = my_rank[None, :] == slot_range[:, None]
    selector = (select_home[:, None, :] & select_rank[None, :, :]).astype(jnp.bfloat16)
    picked = jnp.einsum("ktc,kcd->td", incoming, selector, preferred_element_type=jnp.float32)
    full_hidden, full_gain = (
        lax.all_gather(hidden, "voc", axis=1, tiled=True),
        lax.all_gather(gain, "voc", axis=0, tiled=True),
    )
    hidden_wide = full_hidden.astype(jnp.float32)
    gain_wide = full_gain.astype(jnp.float32)
    full_width = hidden_wide.shape[1]
    inv_scale = lax.rsqrt(jnp.mean(hidden_wide * hidden_wide, axis=1) + epsilon)
    normed = (hidden_wide * inv_scale[:, None] * gain_wide[None, :]).astype(jnp.bfloat16)
    draft_logits = jnp.dot(normed, head_weight, preferred_element_type=jnp.float32)
    top_draft = jnp.max(draft_logits, axis=1)
    total_draft = jnp.sum(jnp.exp(draft_logits - top_draft[:, None]), axis=1)
    top_picked = jnp.max(picked, axis=1)
    lifted = jnp.exp(picked - top_picked[:, None])
    merged = joined(
        (
            top_target,
            total_target,
            top_picked,
            jnp.sum(lifted, axis=1),
            jnp.sum(lifted * draft_logits, axis=1),
            top_draft,
            total_draft,
        ),
        "voc",
        joined_merge,
    )
    target_lse = merged[0] + jnp.log(merged[1])
    factor = jnp.exp(merged[2] - target_lse)
    draft_mass = merged[3] * factor
    cross_term = merged[4] * factor
    top_draft = merged[5]
    total_draft = merged[6]
    target_probs = jnp.exp(picked - target_lse[:, None])
    draft_lse = top_draft + jnp.log(total_draft)
    token_loss = weight * (draft_mass * draft_lse - cross_term)
    soft_probs = jnp.exp(draft_logits - draft_lse[:, None])
    grad_logits = (weight[:, None] * (draft_mass[:, None] * soft_probs - target_probs)).astype(
        jnp.bfloat16
    )
    cubed = inv_scale * inv_scale * inv_scale
    grad_terms = lax.dot_general(
        grad_logits, head_weight, (((1,), (1,)), ((), ())), preferred_element_type=jnp.float32
    )
    grad_normed = lax.psum(grad_terms, "voc")
    inner_sum = jnp.sum(hidden_wide * gain_wide[None, :] * grad_normed, axis=1)
    full_grad = (
        gain_wide[None, :] * inv_scale[:, None] * grad_normed
        - hidden_wide * (cubed * inner_sum / full_width)[:, None]
    )
    d_hidden = lax.dynamic_slice_in_dim(full_grad, shard_id * part_width, part_width, 1)
    return (d_hidden, token_loss)


def solution(mesh):
    in_specs = (P("tok", "voc"), P("tok", "voc"), P("voc"), P(None, "voc"), P(), P("tok"))
    out_specs = (P("tok", "voc"), P("tok"))
    return jax.shard_map(
        per_device, mesh=mesh, in_specs=in_specs, out_specs=out_specs, check_vma=False
    )
```

profile of v0, /device:TPU:64, one launch (start us, length us, event | category | flops | bytes accessed | tf_op | source)
XLA Modules:
  0.0 361.3 jit_solution(6643213271831294757)
XLA Ops:
  10.3 2.3 select_reduce_fusion
  12.6 23.8 %while.32 = (s32[]{:T(128)}, bf16[16,128,152]{1,2,0:T(8,128)(2,1)}, s32[16,152]{1,0:T(8,128)S(1)}, bf16[128,8016]{0,1:T(8,128)(2,1)S(1)}, s32[]{:T(128)}) while((s32[]{:T(128)}, bf16[16,128,152]{1,2,0:T(8,128)(2,1)}, s32[16,152]{1,0:T(8,128)S(1)}, bf16[128,8016]{0,1:T(8,128)(2,1)S(1)}, s32[]{:T(128)}) %tuple.66), condition=%wide.region_9.10_spmd, body=%wide.region_8.9_spmd.sunk | while | flops 313156480 | bytes 2093409 | solution.py:83
  21.5 1.5 fusion.75
  24.5 1.5 fusion.75
  29.0 1.5 fusion.75
  34.9 1.5 fusion.75
  36.4 7.2 %all-to-all-start = ((bf16[16,128,152]{1,2,0:T(8,128)(2,1)}), bf16[16,128,152]{1,2,0:T(8,128)(2,1)S(1)}, u32[]{:S(2)}, u32[]{:S(2)}) async-start(bf16[16,128,152]{1,2,0:T(8,128)(2,1)} %get-tuple-element.107), calls=%async_computation | async-start | bytes 1245184 | tf_op jit(solution)/shard_map/all_to_all | solution.py:84
  46.5 21.4 %all-gather.9 = f32[16,1,128]{2,1,0:T(1,128)S(1)} all-gather(f32[1,1,128]{2,1,0:T(1,128)S(1)} %bitcast.151), channel_id=3, replica_groups=mesh['tok'=16,'voc'=16] {'voc'}, dimensions={0}, use_global_device_ids=true | all-gather | bytes 8704 | tf_op jit(solution)/shard_map/all_gather | solution.py:10
  67.9 19.4 %all-gather.8 = f32[16,1,128]{2,1,0:T(1,128)S(1)} all-gather(f32[1,1,128]{2,1,0:T(1,128)S(1)} %get-tuple-element.172), channel_id=2, replica_groups=mesh['tok'=16,'voc'=16] {'voc'}, dimensions={0}, use_global_device_ids=true | all-gather | bytes 8704 | tf_op jit(solution)/shard_map/all_gather | solution.py:10
  89.1 21.8 %psum.14 = f32[]{:T(128)} all-reduce(f32[]{:T(128)} %convert_reduce_fusion), channel_id=1, replica_groups=mesh['tok'=16,'voc'=16] {'tok'}, use_global_device_ids=true, to_apply=%region_3.0 | all-reduce | flops 1 | bytes 8 | tf_op jit(solution)/shard_map/psum | solution.py:54
  110.9 21.3 %all-gather.7 = bf16[16,1,256]{2,1,0:T(2,128)(2,1)S(1)} all-gather(bf16[1,1,256]{2,1,0:T(2,128)(2,1)S(1)} %reshape.160), channel_id=1, replica_groups=mesh['tok'=16,'voc'=16] {'voc'}, dimensions={0}, use_global_device_ids=true | all-gather | bytes 8704 | tf_op jit(solution)/shard_map/all_gather | solution.py:93
  133.1 2.8 fusion.63
  135.9 19.6 %all-gather.10 = f32[16,1,128]{2,1,0:T(1,128)S(1)} all-gather(f32[1,1,128]{2,1,0:T(1,128)S(1)} %bitcast.147), channel_id=4, replica_groups=mesh['tok'=16,'voc'=16] {'voc'}, dimensions={0}, use_global_device_ids=true | all-gather | bytes 8704 | tf_op jit(solution)/shard_map/all_gather | solution.py:10
  155.5 1.5 multiply_reduce_fusion.1
  157.1 5.2 %fusion.64 = (f32[128]{0:T(128)S(1)}, f32[128,1000]{0,1:T(8,128)S(1)}) fusion(bf16[4096,1000]{0,1:T(8,128)(2,1)} %param.13, bf16[128,4096]{1,0:T(8,128)(2,1)} %all-gather.17.cloned.1.call-done, f32[128]{0:T(128)S(1)} %add_rsqrt_fusion, f32[4096]{0:T(1024)S(1)} %bitcast.133), kind=kOutput, calls=%fused_computation.112 | convolution fusion | flops 1050801024 | bytes 9769984 | tf_op jit(solution)/shard_map/dot_general | solution.py:100
  162.5 18.3 %all-gather.14 = f32[16,1,128]{2,1,0:T(1,128)S(1)} all-gather(f32[1,1,128]{2,1,0:T(1,128)S(1)} %bitcast.150), channel_id=8, replica_groups=mesh['tok'=16,'voc'=16] {'voc'}, dimensions={0}, use_global_device_ids=true | all-gather | bytes 8704 | tf_op jit(solution)/shard_map/all_gather | solution.py:10
  180.8 20.3 %all-gather.12 = f32[16,1,128]{2,1,0:T(1,128)S(1)} all-gather(f32[1,1,128]{2,1,0:T(1,128)S(1)} %bitcast.149), channel_id=6, replica_groups=mesh['tok'=16,'voc'=16] {'voc'}, dimensions={0}, use_global_device_ids=true | all-gather | bytes 8704 | tf_op jit(solution)/shard_map/all_gather | solution.py:10
  201.1 18.2 %all-gather.11 = f32[16,1,128]{2,1,0:T(1,128)S(1)} all-gather(f32[1,1,128]{2,1,0:T(1,128)S(1)} %bitcast.148), channel_id=5, replica_groups=mesh['tok'=16,'voc'=16] {'voc'}, dimensions={0}, use_global_device_ids=true | all-gather | bytes 8704 | tf_op jit(solution)/shard_map/all_gather | solution.py:10
  219.3 20.3 %all-gather.13 = f32[16,1,128]{2,1,0:T(1,128)S(1)} all-gather(f32[1,1,128]{2,1,0:T(1,128)S(1)} %bitcast.146), channel_id=7, replica_groups=mesh['tok'=16,'voc'=16] {'voc'}, dimensions={0}, use_global_device_ids=true | all-gather | bytes 8704 | tf_op jit(solution)/shard_map/all_gather | solution.py:10
  239.7 1.7 while.33
  241.9 6.2 %fusion.49 = f32[128,4096]{1,0:T(8,128)} fusion(bf16[4096,1000]{0,1:T(8,128)(2,1)} %param.13, f32[128,1000]{0,1:T(8,128)S(1)} %get-tuple-element.174, f32[128,1000]{0,1:T(8,128)S(1)} %get-tuple-element.176, f32[128]{0:T(128)S(1)} %get-tuple-element.165, f32[128]{0:T(128)S(1)} %get-tuple-element.164, f32[128]{0:T(128)S(1)} %fusion.58, ...), kind=kOutput, calls=%fused_computation.65 | convolution fusion | flops 1049344000 | bytes 11315200 | tf_op jit(solution)/shard_map/dot_general | solution.py:132
  249.6 101.2 %all-reduce.2.cloned.1.call-done = f32[128,4096]{1,0:T(8,128)} async-done(((f32[128,4096]{1,0:T(8,128)}), f32[128,4096]{1,0:T(8,128)}) %all-reduce.2.cloned.1.call-update) | async-done | bytes 2097168 | tf_op jit(solution)/shard_map/psum | solution.py:135
  350.8 1.9 multiply_reduce_fusion
  352.8 1.7 fusion.54
  (152 shorter events, 29.4 us)
Async XLA Ops:
  7.2 5.4 %copy-start.1 = (bf16[128,8016]{0,1:T(8,128)(2,1)S(1)}, bf16[128,8016]{0,1:T(8,128)(2,1)}, u32[]{:S(2)}) copy-start(bf16[128,8016]{0,1:T(8,128)(2,1)} %param.10) | copy-start | bytes 6156292
  36.4 50.9 %copy-start.2 = (s32[16000]{0:T(1024)S(1)}, s32[16000]{0:T(1024)}, u32[]{:S(2)}) copy-start(s32[16000]{0:T(1024)} %param.14) | copy-start | bytes 192004
  36.4 50.9 %copy-start.3 = (s32[128]{0:T(128)S(1)}, s32[128]{0:T(128)}, u32[]{:S(2)}) copy-start(s32[128]{0:T(128)} %param.15) | copy-start | bytes 1540
  36.4 74.5 %copy-start.4 = (bf16[256]{0:T(256)(128)(2,1)S(1)}, bf16[256]{0:T(256)(128)(2,1)}, u32[]{:S(2)}) copy-start(bf16[256]{0:T(256)(128)(2,1)} %param.12) | copy-start | bytes 1540
  36.4 96.7 %all-to-all-start = ((bf16[16,128,152]{1,2,0:T(8,128)(2,1)}), bf16[16,128,152]{1,2,0:T(8,128)(2,1)S(1)}, u32[]{:S(2)}, u32[]{:S(2)}) async-start(bf16[16,128,152]{1,2,0:T(8,128)(2,1)} %get-tuple-element.107), calls=%async_computation | async-start | bytes 1245184 | tf_op jit(solution)/shard_map/all_to_all | solution.py:84
  43.6 111.9 %all-gather.17.cloned.1.call-start = ((), (), s32[]{:S(2)}) async-start(), calls=%async_computation.1 | async-start | bytes 1114112 | tf_op jit(solution)/shard_map/all_gather | solution.py:92
  44.3 306.5 %all-reduce.2.cloned.1.call-start = ((), (), s32[]{:S(2)}) async-start(), calls=%async_computation.2 | async-start | bytes 4194304 | tf_op jit(solution)/shard_map/psum | solution.py:135
  248.2 1.2 copy-start
Sparse Core Ops, SparseCore 0:
  46.8 50.7 all-gather.16
  248.3 102.4 all-reduce.1
where the time goes:
time: 362 us; the launch traced here: 361 us
  blocking collectives  181 us (50%)
  waiting for transfers between devices  102 us (28%)
  matrix products  38.8 us (11%)
  other arithmetic  15.7 us (4%)
  between operations  14.9 us (4%)
  starting transfers between devices  7.24 us (2%)
    all_gather x7, blocking collectives, joined(): pieces = jax.tree.map(lambda part: lax.all_gather(part, axis), value)  138 us
    psum x1, waiting for transfers between devices, per_device(): grad_normed = lax.psum(grad_terms, 'voc')  101 us
    dot_general x16, matrix products, pick_block(): jnp.dot(target_logits, one_hot, preferred_element_type=jnp.float32)  23.7 us
    psum x1, blocking collectives, per_device(): valid_total = lax.psum(jnp.sum(inside), 'tok')  21.8 us
    all_gather x1, blocking collectives, per_device(): lax.all_gather(gain, 'voc', axis=0, tiled=True)  21.3 us
  transfers between devices with their start and end apart: 3, of which 1 were waited for; matrix products, arithmetic and copies ran while one was open for 2% of the time, Pallas kernels for 0%

commit v1 on v0

v1 whole, which is shorter than its diff:
```python
import functools
import jax
import jax.numpy as jnp
from jax import lax
from jax.experimental import pallas as pl
from jax.experimental.pallas import tpu as pltpu
from jax.sharding import PartitionSpec as P

epsilon = 1e-05
MESH = pl.DeviceIdType.MESH
f32 = jnp.float32
bf16 = jnp.bfloat16
NT = (((1,), (1,)), ((), ()))


def up(value, unit):
    return -(-value // unit) * unit


def body(
    dims,
    ids_ref,
    tok_ref,
    hid_ref,
    gain_ref,
    x_hbm,
    w_hbm,
    dh_ref,
    loss_ref,
    x_v,
    w_v,
    hall,
    nrm,
    table,
    stage,
    psend,
    precv,
    pwide,
    key_v,
    col_v,
    slot_f,
    slot_v,
    slot_s,
    idx_v,
    idx_s,
    logits,
    lt,
    pt,
    grad_t,
    stats,
    count,
    gsend,
    grecv,
    local_sem,
    h_send,
    h_recv,
    p_send,
    p_recv,
    s_send,
    s_recv,
    c_send,
    c_recv,
    g_send,
    g_recv,
):
    n, m, vd, dv, cap = dims
    rows, part = hid_ref.shape
    width = n * part
    dp = ids_ref.shape[1]
    slots = psend.shape[1]
    i = lax.axis_index("tok")
    j = lax.axis_index("voc")

    copy_x = pltpu.make_async_copy(x_hbm, x_v, local_sem.at[0])
    copy_w = pltpu.make_async_copy(w_hbm, w_v, local_sem.at[1])
    copy_x.start()
    copy_w.start()

    barrier = pltpu.get_barrier_semaphore()

    def greet_voc(step, _):
        peer = lax.rem(j + step, n)
        pl.semaphore_signal(barrier, inc=1, device_id=(i, peer), device_id_type=MESH)
        return 0

    def greet_tok(step, _):
        peer = lax.rem(i + step, m)
        pl.semaphore_signal(barrier, inc=1, device_id=(peer, j), device_id_type=MESH)
        return 0

    lax.fori_loop(1, n, greet_voc, 0)
    lax.fori_loop(1, m, greet_tok, 0)

    hall[j, 0:rows, :] = hid_ref[...]
    hall[j, rows : rows + 16, :] = jnp.broadcast_to(
        gain_ref[...].astype(f32), (16, part)
    ).astype(bf16)

    pl.semaphore_wait(barrier, n + m - 2)

    def h_copy(slot, peer):
        return pltpu.make_async_remote_copy(
            src_ref=hall.at[j],
            dst_ref=hall.at[slot],
            send_sem=h_send.at[peer],
            recv_sem=h_recv.at[slot],
            device_id=(i, peer),
            device_id_type=MESH,
        )

    def h_start(step, _):
        h_copy(j, lax.rem(j + step, n)).start()
        return 0

    lax.fori_loop(1, n, h_start, 0)

    ids = ids_ref[...]
    low = (j * vd).astype(f32)
    mine = (ids >= low) & (ids < low + vd)
    own = ids_ref[pl.ds(j, 1), :]
    home = jnp.zeros_like(own)
    for k in range(1, n):
        home += (own >= float(k * vd)).astype(f32)
    shard_row = lax.broadcasted_iota(jnp.int32, (n, dp), 0).astype(f32)
    hit = (shard_row == home).astype(f32)
    before = (
        lax.broadcasted_iota(jnp.int32, (dp, dp), 0)
        < lax.broadcasted_iota(jnp.int32, (dp, dp), 1)
    ).astype(f32).astype(bf16)
    rank_mine = jnp.dot(mine.astype(f32).astype(bf16), before, preferred_element_type=f32)
    rank_hit = jnp.dot(hit.astype(bf16), before, preferred_element_type=f32)
    rank_own = jnp.sum(rank_hit * hit, axis=0, keepdims=True)
    key_v[...] = jnp.where(mine, rank_mine, -1.0)
    col_v[...] = ids - low
    idx_v[...] = jnp.clip(
        jnp.broadcast_to(home * slots + rank_own, idx_v.shape).astype(jnp.int32), 0, n * slots - 1
    )

    slot_row = lax.broadcasted_iota(jnp.int32, (slots, dp), 0).astype(f32)
    slot_lane = lax.broadcasted_iota(jnp.int32, (slots, 128), 1)

    def slot_step(k, acc):
        keys = key_v[pl.ds(k, 1), :]
        cols = col_v[pl.ds(k, 1), :]
        found = jnp.sum(jnp.where(slot_row == keys, cols, 0.0), axis=1, keepdims=True)
        return jnp.where(slot_lane == k, found, acc)

    slot_f[...] = jnp.zeros_like(slot_f)
    slot_f[0:slots, :] = lax.fori_loop(0, n, slot_step, jnp.zeros((slots, 128), f32))
    slot_v[...] = jnp.clip(slot_f[...].T[0:n, :].astype(jnp.int32), 0, vd - 1)
    copy_slot = pltpu.make_async_copy(slot_v, slot_s, local_sem.at[2])
    copy_idx = pltpu.make_async_copy(idx_v, idx_s, local_sem.at[3])
    copy_slot.start()
    copy_idx.start()

    token_rows = jnp.broadcast_to(tok_ref[...], (rows, rows)).T

    def valid_step(k, acc):
        entries = ids_ref[pl.ds(k, 1), :]
        for c in range(dp // 128):
            acc = jnp.where(entries[:, c * 128 : (c + 1) * 128] == token_rows, 1.0, acc)
        return acc

    valid = lax.fori_loop(0, n, valid_step, jnp.zeros((rows, 128), f32))
    valid = jnp.max(valid.T, axis=0, keepdims=True)
    count[i] = jnp.broadcast_to(jnp.sum(valid, axis=1, keepdims=True), (8, 128))

    def c_copy(slot, peer):
        return pltpu.make_async_remote_copy(
            src_ref=count.at[i],
            dst_ref=count.at[slot],
            send_sem=c_send.at[peer],
            recv_sem=c_recv.at[slot],
            device_id=(peer, j),
            device_id_type=MESH,
        )

    def c_start(step, _):
        c_copy(i, lax.rem(i + step, m)).start()
        return 0

    lax.fori_loop(1, m, c_start, 0)

    copy_x.wait()
    piece = 256
    whole = vd // piece
    tail = vd - whole * piece
    eye = (
        lax.broadcasted_iota(jnp.int32, (piece, piece), 0)
        == lax.broadcasted_iota(jnp.int32, (piece, piece), 1)
    ).astype(f32).astype(bf16)

    def turn(c, _):
        at = pl.multiple_of(c * piece, piece)
        table[pl.ds(at, piece), :] = lax.dot_general(
            eye, x_v[:, pl.ds(at, piece)], NT, preferred_element_type=f32
        )
        return 0

    lax.fori_loop(0, whole, turn, 0)
    if tail:
        table[whole * piece : vd, :] = lax.dot_general(
            eye[0:tail, 0:tail], x_v[:, whole * piece : vd], NT, preferred_element_type=f32
        )

    copy_slot.wait()
    copy_idx.wait()
    stage[...] = jnp.zeros_like(stage)

    def p_copy(slot, peer):
        return pltpu.make_async_remote_copy(
            src_ref=psend.at[peer],
            dst_ref=precv.at[slot],
            send_sem=p_send.at[peer],
            recv_sem=p_recv.at[slot],
            device_id=(i, peer),
            device_id_type=MESH,
        )

    def pick(k):
        def pick_rows(q, _):
            for u in range(8):
                at = q * 8 + u
                entry = jnp.clip(slot_s[k, at], 0, vd - 1)
                stage[pl.ds(at, 1), :] = table[pl.ds(entry, 1), :]
            return 0

        lax.fori_loop(0, cap // 8, pick_rows, 0)
        return stage[...].astype(bf16)

    def pick_step(step, _):
        peer = lax.rem(j + step, n)
        psend[peer] = pick(peer)
        p_copy(j, peer).start()
        return 0

    lax.fori_loop(1, n, pick_step, 0)
    precv[j] = pick(j)

    parts = 6
    span = vd // parts
    top_target = lax.fori_loop(
        0,
        parts,
        lambda c, top: jnp.maximum(
            top, jnp.max(table[pl.ds(pl.multiple_of(c * span, 8), span), :], axis=0, keepdims=True)
        ),
        jnp.full((1, rows), -1e30, f32),
    )
    total_target = lax.fori_loop(
        0,
        parts,
        lambda c, total: total
        + jnp.sum(
            jnp.exp(table[pl.ds(pl.multiple_of(c * span, 8), span), :] - top_target),
            axis=0,
            keepdims=True,
        ),
        jnp.zeros((1, rows), f32),
    )

    def h_wait(step, _):
        h_copy(lax.rem(j + step, n), j).wait_recv()
        return 0

    lax.fori_loop(1, n, h_wait, 0)

    def square(k, acc):
        wide = hall[k, 0:rows, :].astype(f32)
        return acc + wide * wide

    squares = lax.fori_loop(0, n, square, jnp.zeros((rows, part), f32))
    inv = lax.rsqrt(jnp.sum(squares, axis=1, keepdims=True) / width + epsilon)

    def normalise(k, _):
        wide = hall[k, 0:rows, :].astype(f32)
        gains = hall[k, rows : rows + 16, :].astype(f32)[0:1, :]
        at = pl.multiple_of(k * part, part)
        nrm[:, pl.ds(at, part)] = (wide * inv * gains).astype(bf16)
        return 0

    lax.fori_loop(0, n, normalise, 0)
    inv_row = jnp.broadcast_to(inv, (rows, 128)).T[0:1, :]

    copy_w.wait()
    logits[:, 0:dv] = jnp.dot(nrm[...], w_v[...], preferred_element_type=f32)
    lt[...] = logits[...].T
    draft = lt[0:dv, :]
    top_draft = jnp.max(draft, axis=0, keepdims=True)
    lifted = jnp.exp(draft - top_draft)
    total_draft = jnp.sum(lifted, axis=0, keepdims=True)
    cross_draft = jnp.sum(lifted * draft, axis=0, keepdims=True)

    def p_wait(step, _):
        p_copy(lax.rem(j + step, n), j).wait_recv()
        return 0

    lax.fori_loop(1, n, p_wait, 0)

    def widen(k, _):
        pwide[pl.ds(pl.multiple_of(k * slots, 8), slots), :] = precv[k].astype(f32)
        return 0

    lax.fori_loop(0, n, widen, 0)

    def place(q, _):
        for u in range(8):
            at = q * 8 + u
            entry = jnp.clip(idx_s[0, at], 0, n * slots - 1)
            pt[pl.ds(at, 1), :] = pwide[pl.ds(entry, 1), :]
        return 0

    lax.fori_loop(0, dv // 8, place, 0)
    picked = pt[...]
    top_picked = jnp.max(picked, axis=0, keepdims=True)
    raised = jnp.exp(picked - top_picked)
    total_picked = jnp.sum(raised, axis=0, keepdims=True)
    cross_picked = jnp.sum(raised * lt[0:dv, :], axis=0, keepdims=True)

    tops = (top_target, top_picked, top_picked, top_draft, top_draft)
    sums = (total_target, total_picked, cross_picked, total_draft, cross_draft)
    stats[j] = jnp.zeros((16, 128), f32)
    for r in range(5):
        stats[j, r : r + 1, :] = tops[r]
        stats[j, 8 + r : 9 + r, :] = sums[r]

    def s_copy(slot, peer):
        return pltpu.make_async_remote_copy(
            src_ref=stats.at[j],
            dst_ref=stats.at[slot],
            send_sem=s_send.at[peer],
            recv_sem=s_recv.at[slot],
            device_id=(i, peer),
            device_id_type=MESH,
        )

    def s_start(step, _):
        s_copy(j, lax.rem(j + step, n)).start()
        return 0

    def s_wait(step, _):
        s_copy(lax.rem(j + step, n), j).wait_recv()
        return 0

    def c_wait(step, _):
        c_copy(lax.rem(i + step, m), i).wait_recv()
        return 0

    lax.fori_loop(1, n, s_start, 0)
    lax.fori_loop(1, m, c_wait, 0)
    valid_total = jnp.sum(count[...], axis=0)[0:1, :]
    weight = valid * (float(rows * m) / valid_total)
    hid_t = hid_ref[...].astype(f32).T
    gain_t = jnp.broadcast_to(gain_ref[...].astype(f32), (rows, part)).T
    lax.fori_loop(1, n, s_wait, 0)

    top = stats[0, 0:8, :]
    for k in range(1, n):
        top = jnp.maximum(top, stats[k, 0:8, :])
    total = jnp.zeros((8, 128), f32)
    for k in range(n):
        total += stats[k, 8:16, :] * jnp.exp(stats[k, 0:8, :] - top)
    target_lse = top[0:1, :] + jnp.log(total[0:1, :])
    factor = jnp.exp(top[1:2, :] - target_lse)
    mass = total[1:2, :] * factor
    cross = total[2:3, :] * factor
    draft_lse = top[3:4, :] + jnp.log(total[3:4, :])
    loss_ref[...] = weight * (mass * draft_lse - cross)
    spread = weight * (mass * (total[4:5, :] / total[3:4, :]) - cross)
    shrink = inv_row * inv_row * spread / width

    soft = jnp.exp(lt[0:dv, :] - draft_lse)
    probs = jnp.exp(pt[...] - target_lse)
    grad_t[...] = (weight * (mass * soft - probs)).astype(bf16)

    def g_copy(slot, peer):
        return pltpu.make_async_remote_copy(
            src_ref=gsend.at[peer],
            dst_ref=grecv.at[slot],
            send_sem=g_send.at[peer],
            recv_sem=g_recv.at[slot],
            device_id=(i, peer),
            device_id_type=MESH,
        )

    def term(k):
        at = pl.multiple_of(k * part, part)
        return jnp.dot(w_v[pl.ds(at, part), :], grad_t[...], preferred_element_type=f32)

    def g_step(step, _):
        peer = lax.rem(j + step, n)
        gsend[peer] = term(peer).astype(bf16)
        g_copy(j, peer).start()
        return 0

    lax.fori_loop(1, n, g_step, 0)

    def g_sum(step, acc):
        slot = lax.rem(j + step, n)
        g_copy(slot, j).wait_recv()
        return acc + grecv[slot].astype(f32)

    grad_normed = lax.fori_loop(1, n, g_sum, term(j))
    dh_ref[...] = (gain_t * inv_row * grad_normed - hid_t * shrink).T

    def finish_voc(step, _):
        peer = lax.rem(j + step, n)
        h_copy(j, peer).wait_send()
        p_copy(j, peer).wait_send()
        s_copy(j, peer).wait_send()
        g_copy(j, peer).wait_send()
        return 0

    def finish_tok(step, _):
        c_copy(i, lax.rem(i + step, m)).wait_send()
        return 0

    lax.fori_loop(1, n, finish_voc, 0)
    lax.fori_loop(1, m, finish_tok, 0)


def per_device(target_logits, hidden, gain, head_weight, draft_ids, token_ids):
    n = lax.axis_size("voc")
    m = lax.axis_size("tok")
    rows, part = hidden.shape
    vd = target_logits.shape[1]
    width, dv = head_weight.shape
    cap = 8 * (5 * dv // (16 * n))
    slots = up(cap, 16)
    dp = up(dv, 128)
    slot_lanes = up(slots, 128)
    ids = jnp.pad(
        draft_ids.reshape(n, dv).astype(f32), ((0, 0), (0, dp - dv)), constant_values=-1.0
    )
    tokens = token_ids.astype(f32).reshape(1, rows)
    vmem = pl.BlockSpec(memory_space=pltpu.VMEM)
    anywhere = pl.BlockSpec(memory_space=pl.ANY)
    dma = pltpu.SemaphoreType.DMA
    d_hidden, loss = pl.pallas_call(
        functools.partial(body, (n, m, vd, dv, cap)),
        out_shape=(
            jax.ShapeDtypeStruct((rows, part), f32),
            jax.ShapeDtypeStruct((1, rows), f32),
        ),
        in_specs=[vmem, vmem, vmem, vmem, anywhere, anywhere],
        out_specs=(vmem, vmem),
        scratch_shapes=[
            pltpu.VMEM((rows, vd), bf16),
            pltpu.VMEM((width, dv), bf16),
            pltpu.VMEM((n, rows + 16, part), bf16),
            pltpu.VMEM((rows, width), bf16),
            pltpu.VMEM((vd, rows), f32),
            pltpu.VMEM((slots, rows), f32),
            pltpu.VMEM((n, slots, rows), bf16),
            pltpu.VMEM((n, slots, rows), bf16),
            pltpu.VMEM((n * slots, rows), f32),
            pltpu.VMEM((n, dp), f32),
            pltpu.VMEM((n, dp), f32),
            pltpu.VMEM((slot_lanes, 128), f32),
            pltpu.VMEM((n, slot_lanes), jnp.int32),
            pltpu.SMEM((n, slot_lanes), jnp.int32),
            pltpu.VMEM((8, dp), jnp.int32),
            pltpu.SMEM((8, dp), jnp.int32),
            pltpu.VMEM((rows, dp), f32),
            pltpu.VMEM((dp, rows), f32),
            pltpu.VMEM((dv, rows), f32),
            pltpu.VMEM((dv, rows), bf16),
            pltpu.VMEM((n, 16, 128), f32),
            pltpu.VMEM((m, 8, 128), f32),
            pltpu.VMEM((n, part, rows), bf16),
            pltpu.VMEM((n, part, rows), bf16),
            dma((4,)),
            dma((n,)),
            dma((n,)),
            dma((n,)),
            dma((n,)),
            dma((n,)),
            dma((n,)),
            dma((m,)),
            dma((m,)),
            dma((n,)),
            dma((n,)),
        ],
        compiler_params=pltpu.CompilerParams(
            collective_id=0, has_side_effects=True, vmem_limit_bytes=48 * 1024 * 1024
        ),
    )(ids, tokens, hidden, gain.reshape(1, part), target_logits, head_weight)
    return d_hidden, loss.reshape(rows)


def solution(mesh):
    in_specs = (P("tok", "voc"), P("tok", "voc"), P("voc"), P(None, "voc"), P(), P("tok"))
    out_specs = (P("tok", "voc"), P("tok"))
    return jax.shard_map(
        per_device, mesh=mesh, in_specs=in_specs, out_specs=out_specs, check_vma=False
    )
```

time: 362 us -> 85.7 us (0.24)
  the two profiles are of different devices: /device:TPU:64 before, /device:TPU:1 now
where the time goes in v1:
time: 85.7 us; the launch traced here: 85.2 us
  Pallas kernels  66.2 us (77%)
  local copies, waits for them, and re-layouts  16.8 us (20%)
  other arithmetic  1.5 us (2%)
    pallas_call x1, Pallas kernels, per_device(): pl.pallas_call(functools.partial(body, (n, m, vd, dv, cap)), out_shape=(j...  66.2 us
    unnamed x6, local copies, waits for them, and re-layouts  16 us

profile of v1, /device:TPU:1, one launch (start us, length us, event | category | flops | bytes accessed | tf_op | source)
XLA Modules:
  0.0 85.2 jit_solution(3451776542027357586)
XLA Ops:
  0.6 0.7 convert_bitcast_fusion.tok_ref
  1.3 0.7 reshape.16.gain_ref
  1.9 0.8 convert_element_type.9
  2.8 0.1 convert_element_type.10
  2.9 2.9 %copy.8.x_hbm = bf16[128,8016]{1,0:T(8,128)(2,1)S(1)} copy(bf16[128,8016]{0,1:T(8,128)(2,1)} %param.6) | data formatting | bytes 4104192 | tf_op args[0]
  5.8 0.0 copy-start
  5.8 12.0 %copy.9.w_hbm = bf16[4096,1000]{1,0:T(8,128)(2,1)} copy(bf16[4096,1000]{0,1:T(8,128)(2,1)} %param.9) | data formatting | bytes 16384000 | tf_op args[3]
  17.8 0.0 copy-done
  17.8 66.2 %shard_map.77 = (f32[128,256]{1,0:T(8,128)S(1)}, f32[1,128]{1,0:T(1,128)S(1)}) custom-call(f32[16,1024]{1,0:T(8,128)S(1)} %pad.4.ids_ref, f32[1,128]{1,0:T(1,128)S(1)} %convert_bitcast_fusion.tok_ref, bf16[128,256]{1,0:T(8,128)(2,1)S(1)} %copy-done, bf16[1,256]{1,0:T(2,128)(2,1)S(1)} %reshape.16.gain_ref, bf16[128,8016]{1,0:T(8,128)(2,1)S(1)} %copy.8.x_hbm, ...), custom_call_target="tpu_custom_call" | custom-call | tf_op jit(solution)/shard_map/pallas_call | solution.py:439
  84.0 0.7 copy.12
  84.7 0.5 copy.13
  (1 shorter events, 0.0 us)
Async XLA Ops:
  5.8 12.0 %copy-start = (bf16[128,256]{1,0:T(8,128)(2,1)S(1)}, bf16[128,256]{1,0:T(8,128)(2,1)}, u32[]{:S(2)}) copy-start(bf16[128,256]{1,0:T(8,128)(2,1)} %hid_ref.1) | copy-start | bytes 196612

commit v2 on v1

v2 whole, which is shorter than its diff:
```python
import functools
import math
import jax
import jax.numpy as jnp
from jax import lax
from jax.experimental import pallas as pl
from jax.experimental.pallas import tpu as pltpu
from jax.sharding import PartitionSpec as P

epsilon = 1e-05
MESH = pl.DeviceIdType.MESH
f32 = jnp.float32
bf16 = jnp.bfloat16
NT = (((1,), (1,)), ((), ()))


def up(value, unit):
    return -(-value // unit) * unit


def body(
    dims,
    ids_hbm,
    tok_hbm,
    gain_hbm,
    hid_hbm,
    x_hbm,
    w_hbm,
    dh_ref,
    loss_ref,
    ids_v,
    tok_v,
    gain_v,
    x_v,
    w_v,
    hall,
    nrm,
    table,
    stage,
    psend,
    precv,
    pwide,
    idm_v,
    key_v,
    col_v,
    slot_f,
    slot_v,
    slot_s,
    idx_v,
    idx_s,
    lt,
    pt,
    wide_grad,
    grad,
    stat_x,
    stat_y,
    count_out,
    count_in,
    gsend,
    own_a,
    own_b,
    g1a,
    g1b,
    send_a,
    send_b,
    g2a,
    g2b,
    local_sem,
    entered,
    ha_first,
    hb_first,
    ha_next,
    hb_next,
    ha_recv,
    hb_recv,
    p_send,
    p_recv,
    sx_send,
    sx_recv,
    sy_send,
    sy_recv,
    c_send,
    c_recv,
    ga_send,
    gb_send,
    g1a_recv,
    g1b_recv,
    g2a_send,
    g2b_send,
    g2a_recv,
    g2b_recv,
):
    n, m, vd, dv, cap = dims
    side = math.isqrt(n)
    bits = m.bit_length() - 1
    part = hall.shape[2]
    rows = nrm.shape[0]
    half = rows // 2
    width = n * part
    chunks = idx_v.shape[0]
    slots = psend.shape[1]
    i = lax.axis_index("tok")
    j = lax.axis_index("voc")
    x = j // side
    y = lax.rem(j, side)

    def along_x(step):
        return lax.rem(x + step, side)

    def along_y(step):
        return lax.rem(y + step, side)

    def partner(bit):
        return i + (1 - 2 * lax.rem(i // 2**bit, 2)) * 2**bit

    copy_ids = pltpu.make_async_copy(ids_hbm, ids_v, local_sem.at[0])
    copy_hid = pltpu.make_async_copy(hid_hbm, hall.at[j, 0:rows], local_sem.at[1])
    copy_gain = pltpu.make_async_copy(gain_hbm, gain_v, local_sem.at[2])
    copy_tok = pltpu.make_async_copy(tok_hbm, tok_v, local_sem.at[3])
    copy_x = pltpu.make_async_copy(x_hbm, x_v, local_sem.at[4])
    copy_w = pltpu.make_async_copy(w_hbm, w_v, local_sem.at[5])
    copy_ids.start()
    copy_hid.start()
    copy_gain.start()
    copy_tok.start()
    copy_x.start()
    copy_w.start()

    barrier = pltpu.get_barrier_semaphore()

    def greet(step, _):
        for peer in (along_x(step) * side + y, x * side + along_y(step)):
            pl.semaphore_signal(barrier, inc=1, device_id=(i, peer), device_id_type=MESH)
        return 0

    lax.fori_loop(1, side, greet, 0)
    for bit in range(bits):
        pl.semaphore_signal(barrier, inc=1, device_id=(partner(bit), j), device_id_type=MESH)

    copy_ids.wait()
    lane = lax.broadcasted_iota(jnp.int32, (chunks, 128), 1)
    entry = lax.broadcasted_iota(jnp.int32, (chunks, 128), 0) * 128 + lane
    total_rows = ids_v.shape[0]
    for k in range(n):
        first, shift = divmod(k * dv, 128)
        piece = ids_v[first : min(first + chunks + 1, total_rows), :].astype(f32)
        if shift:
            piece = pltpu.roll(piece, 128 - shift, 1)
        if piece.shape[0] == chunks:
            piece = jnp.concatenate([piece, piece[0:1, :]], axis=0)
        early = jnp.where(lane < 128 - shift, piece[0:chunks, :], piece[1 : chunks + 1, :])
        idm_v[k * chunks : (k + 1) * chunks, :] = jnp.where(entry < dv, early, -1.0)
    ids = idm_v[...]
    low = (j * vd).astype(f32)
    mine = ((ids >= low) & (ids < low + vd)).astype(f32)
    own = idm_v[pl.ds(pl.multiple_of(j * chunks, chunks), chunks), :]
    home = jnp.zeros_like(own)
    for k in range(1, n):
        home += (own >= float(k * vd)).astype(f32)
    home_all = jnp.concatenate([home] * n, axis=0)
    tall = (n * chunks, 128)
    row_shard = (lax.broadcasted_iota(jnp.int32, tall, 0) // chunks).astype(f32)
    hit = (home_all == row_shard).astype(f32)
    before = (
        lax.broadcasted_iota(jnp.int32, (128, 128), 0)
        < lax.broadcasted_iota(jnp.int32, (128, 128), 1)
    ).astype(f32).astype(bf16)
    ones = jnp.ones((128, 128), bf16)
    square_rows = (n * chunks, n * chunks)
    at_row = lax.broadcasted_iota(jnp.int32, square_rows, 0)
    at_column = lax.broadcasted_iota(jnp.int32, square_rows, 1)
    earlier = (
        (at_column < at_row) & (at_column >= at_row - at_row % chunks)
    ).astype(f32).astype(bf16)

    def ranks(mask):
        mask = mask.astype(bf16)
        ahead = jnp.dot(earlier, mask, preferred_element_type=f32).astype(bf16)
        return jnp.dot(mask, before, preferred_element_type=f32) + jnp.dot(
            ahead, ones, preferred_element_type=f32
        )

    key_v[...] = jnp.where(mine > 0.5, ranks(mine), -1.0)
    col_v[...] = ids - low
    rank_hit = ranks(hit) * hit
    rank_own = rank_hit[0:chunks, :]
    for k in range(1, n):
        rank_own += rank_hit[k * chunks : (k + 1) * chunks, :]
    idx_v[...] = jnp.clip((home * slots + rank_own).astype(jnp.int32), 0, n * slots - 1)

    copy_hid.wait()
    copy_gain.wait()
    wide_gain = gain_v[...].astype(f32)
    wide_gain = jnp.concatenate([wide_gain[r : r + 1, :] for r in range(part // 128)], axis=1)
    hall[j, rows : rows + 16, :] = jnp.broadcast_to(wide_gain, (16, part)).astype(bf16)

    pl.semaphore_wait(barrier, 2 * (side - 1) + bits)

    def ha_copy(block, to_x, to_y, send_sem):
        piece = hall.at[block, 0:half]
        return pltpu.make_async_remote_copy(
            src_ref=piece,
            dst_ref=piece,
            send_sem=send_sem,
            recv_sem=ha_recv.at[block],
            device_id=(i, to_x * side + to_y),
            device_id_type=MESH,
        )

    def hb_copy(block, to_x, to_y, send_sem):
        piece = hall.at[block, half : rows + 16]
        return pltpu.make_async_remote_copy(
            src_ref=piece,
            dst_ref=piece,
            send_sem=send_sem,
            recv_sem=hb_recv.at[block],
            device_id=(i, to_x * side + to_y),
            device_id_type=MESH,
        )

    def ha_forward(from_x, step):
        to_y = along_y(step)
        return ha_copy(from_x * side + y, x, to_y, ha_next.at[from_x, to_y])

    def hb_forward(from_y, step):
        to_x = along_x(step)
        return hb_copy(x * side + from_y, to_x, y, hb_next.at[from_y, to_x])

    def h_first(step, _):
        ha_copy(j, along_x(step), y, ha_first.at[along_x(step)]).start()
        hb_copy(j, x, along_y(step), hb_first.at[along_y(step)]).start()
        return 0

    def h_own(step, _):
        ha_forward(x, step).start()
        hb_forward(y, step).start()
        pl.semaphore_signal(
            entered, inc=1, device_id=(i, x * side + along_y(step)), device_id_type=MESH
        )
        return 0

    lax.fori_loop(1, side, h_first, 0)
    lax.fori_loop(1, side, h_own, 0)

    slot_row = lax.broadcasted_iota(jnp.int32, (slots, 128), 0).astype(f32)
    slot_lane = lax.broadcasted_iota(jnp.int32, (slots, 128), 1)

    def slot_step(k, acc):
        at = pl.multiple_of(k * chunks, chunks)
        keys = key_v[pl.ds(at, chunks), :]
        cols = col_v[pl.ds(at, chunks), :]
        found = jnp.zeros((slots, 128), f32)
        for c in range(chunks):
            found = jnp.where(slot_row == keys[c : c + 1, :], cols[c : c + 1, :], found)
        return jnp.where(slot_lane == k, jnp.sum(found, axis=1, keepdims=True), acc)

    slot_f[...] = jnp.zeros_like(slot_f)
    slot_f[0:slots, :] = lax.fori_loop(0, n, slot_step, jnp.zeros((slots, 128), f32))
    slot_v[...] = jnp.clip(slot_f[...].T[0:n, :].astype(jnp.int32), 0, vd - 1)
    copy_slot = pltpu.make_async_copy(slot_v, slot_s, local_sem.at[6])
    copy_idx = pltpu.make_async_copy(idx_v, idx_s, local_sem.at[7])
    copy_slot.start()
    copy_idx.start()

    def h_pass(step, _):
        from_x = along_x(step)
        from_y = along_y(step)
        ha_forward(from_x, 1).wait_recv()
        for later in range(1, side):
            ha_forward(from_x, later).start()
        hb_forward(from_y, 1).wait_recv()
        for later in range(1, side):
            hb_forward(from_y, later).start()
        return 0

    lax.fori_loop(1, side, h_pass, 0)

    copy_tok.wait()
    token_rows = jnp.broadcast_to(tok_v[...].astype(f32), (rows, rows)).T

    def valid_step(k, acc):
        entries = idm_v[pl.ds(pl.multiple_of(k * chunks, chunks), chunks), :]
        for c in range(chunks):
            acc = jnp.where(entries[c : c + 1, :] == token_rows, 1.0, acc)
        return acc

    valid = lax.fori_loop(0, n, valid_step, jnp.zeros((rows, 128), f32))
    valid = jnp.max(valid.T, axis=0, keepdims=True)

    def c_copy(bit):
        return pltpu.make_async_remote_copy(
            src_ref=count_out.at[bit],
            dst_ref=count_in.at[bit],
            send_sem=c_send.at[bit],
            recv_sem=c_recv.at[bit],
            device_id=(partner(bit), j),
            device_id_type=MESH,
        )

    def c_start(bit, value):
        count_out[bit] = value
        c_copy(bit).start()

    def c_sum(bit):
        c_copy(bit).wait_recv()
        return count_out[bit] + count_in[bit]

    c_start(0, jnp.broadcast_to(jnp.sum(valid, axis=1, keepdims=True), (8, 128)))

    copy_x.wait()
    parts = 3
    span = vd // parts

    def widen_target(c, top):
        at = pl.multiple_of(c * span, 16)
        wide = x_v[pl.ds(at, span), :].astype(f32)
        table[pl.ds(at, span), :] = wide
        return jnp.maximum(top, jnp.max(wide, axis=0, keepdims=True))

    top_target = lax.fori_loop(0, parts, widen_target, jnp.full((1, rows), -1e30, f32))

    copy_slot.wait()
    copy_idx.wait()
    stage[...] = jnp.zeros_like(stage)

    def p_copy(slot, peer):
        return pltpu.make_async_remote_copy(
            src_ref=psend.at[peer],
            dst_ref=precv.at[slot],
            send_sem=p_send.at[peer],
            recv_sem=p_recv.at[slot],
            device_id=(i, peer),
            device_id_type=MESH,
        )

    def pick(k):
        for at in range(cap):
            stage[at : at + 1, :] = table[pl.ds(slot_s[k, at], 1), :]
        return stage[...].astype(bf16)

    def pick_step(step, _):
        peer = lax.rem(j + step, n)
        psend[peer] = pick(peer)
        p_copy(j, peer).start()
        return 0

    pl.semaphore_wait(entered, side - 1)
    lax.fori_loop(1, n, pick_step, 0)
    precv[j] = pick(j)

    total_target = lax.fori_loop(
        0,
        parts,
        lambda c, total: total
        + jnp.sum(
            jnp.exp(table[pl.ds(pl.multiple_of(c * span, 8), span), :] - top_target),
            axis=0,
            keepdims=True,
        ),
        jnp.zeros((1, rows), f32),
    )
    if bits > 1:
        c_start(1, c_sum(0))

    def h_rest(step, _):
        from_y = along_y(step)

        def h_rest_a(xs, _):
            ha_copy(xs * side + from_y, x, from_y, ha_next.at[0, 0]).wait_recv()
            return 0

        lax.fori_loop(0, side, h_rest_a, 0)
        from_x = along_x(step)

        def h_rest_b(ys, _):
            hb_copy(from_x * side + ys, from_x, y, hb_next.at[0, 0]).wait_recv()
            return 0

        lax.fori_loop(0, side, h_rest_b, 0)
        return 0

    lax.fori_loop(1, side, h_rest, 0)

    def square(k, acc):
        wide = hall[k, 0:rows, :].astype(f32)
        return acc + wide * wide

    squares = lax.fori_loop(0, n, square, jnp.zeros((rows, part), f32))
    inv = lax.rsqrt(jnp.sum(squares, axis=1, keepdims=True) / width + epsilon)

    def normalise(k, _):
        wide = hall[k, 0:rows, :].astype(f32)
        gains = hall[k, rows : rows + 16, :].astype(f32)[0:1, :]
        at = pl.multiple_of(k * part, part)
        nrm[:, pl.ds(at, part)] = (wide * inv * gains).astype(bf16)
        return 0

    lax.fori_loop(0, n, normalise, 0)
    inv_row = jnp.broadcast_to(inv, (rows, 128)).T[0:1, :]
    if bits > 2:
        c_start(2, c_sum(1))

    copy_w.wait()
    lt[...] = lax.dot_general(w_v[...], nrm[...], NT, preferred_element_type=f32)
    draft = lt[...]
    top_draft = jnp.max(draft, axis=0, keepdims=True)
    lifted = jnp.exp(draft - top_draft)
    total_draft = jnp.sum(lifted, axis=0, keepdims=True)
    cross_draft = jnp.sum(lifted * draft, axis=0, keepdims=True)
    if bits > 3:
        c_start(3, c_sum(2))

    def p_wait(step, _):
        p_copy(lax.rem(j + step, n), j).wait_recv()
        return 0

    lax.fori_loop(1, n, p_wait, 0)

    def widen(k, _):
        pwide[pl.ds(pl.multiple_of(k * slots, 8), slots), :] = precv[k].astype(f32)
        return 0

    lax.fori_loop(0, n, widen, 0)
    for at in range(dv):
        pt[at : at + 1, :] = pwide[pl.ds(idx_s[at // 128, at % 128], 1), :]
    picked = pt[...]
    top_picked = jnp.max(picked, axis=0, keepdims=True)
    raised = jnp.exp(picked - top_picked)
    total_picked = jnp.sum(raised, axis=0, keepdims=True)
    cross_picked = jnp.sum(raised * lt[...], axis=0, keepdims=True)

    tops = (top_target, top_picked, top_picked, top_draft, top_draft)
    sums = (total_target, total_picked, cross_picked, total_draft, cross_draft)
    stat_x[x] = jnp.zeros((16, 128), f32)
    for r in range(5):
        stat_x[x, r : r + 1, :] = tops[r]
        stat_x[x, 8 + r : 9 + r, :] = sums[r]

    def sx_copy(slot, to_x):
        return pltpu.make_async_remote_copy(
            src_ref=stat_x.at[slot],
            dst_ref=stat_x.at[slot],
            send_sem=sx_send.at[to_x],
            recv_sem=sx_recv.at[slot],
            device_id=(i, to_x * side + y),
            device_id_type=MESH,
        )

    def sy_copy(slot, to_y):
        return pltpu.make_async_remote_copy(
            src_ref=stat_y.at[slot],
            dst_ref=stat_y.at[slot],
            send_sem=sy_send.at[to_y],
            recv_sem=sy_recv.at[slot],
            device_id=(i, x * side + to_y),
            device_id_type=MESH,
        )

    def merge(ref):
        top = ref[0, 0:8, :]
        for k in range(1, side):
            top = jnp.maximum(top, ref[k, 0:8, :])
        total = jnp.zeros((8, 128), f32)
        for k in range(side):
            total += ref[k, 8:16, :] * jnp.exp(ref[k, 0:8, :] - top)
        return top, total

    for step in range(1, side):
        sx_copy(x, along_x(step)).start()
    valid_total = c_sum(bits - 1)[0:1, :]
    weight = valid * (float(rows * m) / valid_total)
    for step in range(1, side):
        sx_copy(along_x(step), x).wait_recv()
    top, total = merge(stat_x)
    stat_y[y, 0:8, :] = top
    stat_y[y, 8:16, :] = total
    for step in range(1, side):
        sy_copy(y, along_y(step)).start()
    for step in range(1, side):
        sy_copy(along_y(step), y).wait_recv()
    top, total = merge(stat_y)

    target_lse = top[0:1, :] + jnp.log(total[0:1, :])
    factor = jnp.exp(top[1:2, :] - target_lse)
    mass = total[1:2, :] * factor
    cross = total[2:3, :] * factor
    draft_lse = top[3:4, :] + jnp.log(total[3:4, :])
    loss_ref[...] = weight * (mass * draft_lse - cross)
    spread = weight * (mass * (total[4:5, :] / total[3:4, :]) - cross)
    shrink = inv_row * inv_row * spread / width

    soft = jnp.exp(lt[...] - draft_lse)
    probs = jnp.exp(pt[...] - target_lse)
    wide_grad[dv:, :] = jnp.zeros((wide_grad.shape[0] - dv, rows), f32)
    wide_grad[0:dv, :] = weight * (mass * soft - probs)
    grad[...] = wide_grad[...].T.astype(bf16)
    shrink = jnp.broadcast_to(shrink, (rows, rows)).T[:, 0:1]

    def term(to_x, to_y):
        at = pl.multiple_of((to_x * side + to_y) * part, part)
        return jnp.dot(grad[:, 0:dv], w_v[:, pl.ds(at, part)], preferred_element_type=f32)

    def g1a_copy(from_x, to_x, to_y):
        return pltpu.make_async_remote_copy(
            src_ref=gsend.at[to_x, to_y, 0:half],
            dst_ref=g1a.at[from_x, to_y],
            send_sem=ga_send.at[to_x, to_y],
            recv_sem=g1a_recv.at[from_x, to_y],
            device_id=(i, to_x * side + y),
            device_id_type=MESH,
        )

    def g1b_copy(from_y, to_x, to_y):
        return pltpu.make_async_remote_copy(
            src_ref=gsend.at[to_x, to_y, half:rows],
            dst_ref=g1b.at[from_y, to_x],
            send_sem=gb_send.at[to_x, to_y],
            recv_sem=g1b_recv.at[from_y, to_x],
            device_id=(i, x * side + to_y),
            device_id_type=MESH,
        )

    def g_both(t, _):
        to_x = along_x(t // (side - 1) + 1)
        to_y = along_y(t % (side - 1) + 1)
        gsend[to_x, to_y] = term(to_x, to_y).astype(bf16)
        g1a_copy(x, to_x, to_y).start()
        g1b_copy(y, to_x, to_y).start()
        return 0

    def g_column(step, _):
        to_x = along_x(step)
        value = term(to_x, y)
        gsend[to_x, y] = value.astype(bf16)
        g1a_copy(x, to_x, y).start()
        own_b[to_x] = value[half:rows, :]
        return 0

    def g_row(step, _):
        to_y = along_y(step)
        value = term(x, to_y)
        gsend[x, to_y] = value.astype(bf16)
        g1b_copy(y, x, to_y).start()
        own_a[to_y] = value[0:half, :]
        return 0

    lax.fori_loop(0, (side - 1) * (side - 1), g_both, 0)
    lax.fori_loop(1, side, g_column, 0)
    lax.fori_loop(1, side, g_row, 0)
    value = term(x, y)
    own_a[y] = value[0:half, :]
    own_b[x] = value[half:rows, :]

    def sum_a(to_y):
        acc = own_a[to_y]
        for step in range(1, side):
            from_x = along_x(step)
            g1a_copy(from_x, x, to_y).wait_recv()
            acc += g1a[from_x, to_y].astype(f32)
        return acc

    def sum_b(to_x):
        acc = own_b[to_x]
        for step in range(1, side):
            from_y = along_y(step)
            g1b_copy(from_y, to_x, y).wait_recv()
            acc += g1b[from_y, to_x].astype(f32)
        return acc

    def g2a_copy(from_y, to_y):
        return pltpu.make_async_remote_copy(
            src_ref=send_a.at[to_y],
            dst_ref=g2a.at[from_y],
            send_sem=g2a_send.at[to_y],
            recv_sem=g2a_recv.at[from_y],
            device_id=(i, x * side + to_y),
            device_id_type=MESH,
        )

    def g2b_copy(from_x, to_x):
        return pltpu.make_async_remote_copy(
            src_ref=send_b.at[to_x],
            dst_ref=g2b.at[from_x],
            send_sem=g2b_send.at[to_x],
            recv_sem=g2b_recv.at[from_x],
            device_id=(i, to_x * side + y),
            device_id_type=MESH,
        )

    def g_second(step, _):
        to_y = along_y(step)
        send_a[to_y] = sum_a(to_y).astype(bf16)
        g2a_copy(y, to_y).start()
        to_x = along_x(step)
        send_b[to_x] = sum_b(to_x).astype(bf16)
        g2b_copy(x, to_x).start()
        return 0

    lax.fori_loop(1, side, g_second, 0)
    first = sum_a(y)
    second = sum_b(x)
    for step in range(1, side):
        from_y = along_y(step)
        g2a_copy(from_y, y).wait_recv()
        first += g2a[from_y].astype(f32)
        from_x = along_x(step)
        g2b_copy(from_x, x).wait_recv()
        second += g2b[from_x].astype(f32)
    wide_hidden = hall[j, 0:rows, :].astype(f32)
    dh_ref[0:half, :] = (
        wide_gain * inv[0:half, :] * first - wide_hidden[0:half, :] * shrink[0:half, :]
    )
    dh_ref[half:rows, :] = (
        wide_gain * inv[half:rows, :] * second - wide_hidden[half:rows, :] * shrink[half:rows, :]
    )

    def finish_voc(step, _):
        peer = lax.rem(j + step, n)
        p_copy(j, peer).wait_send()
        return 0

    def finish_side(step, _):
        to_x = along_x(step)
        to_y = along_y(step)
        ha_copy(j, to_x, y, ha_first.at[to_x]).wait_send()
        hb_copy(j, x, to_y, hb_first.at[to_y]).wait_send()
        for origin in range(side):
            ha_forward(origin, step).wait_send()
            hb_forward(origin, step).wait_send()
        sx_copy(x, to_x).wait_send()
        sy_copy(y, to_y).wait_send()
        for other in range(side):
            g1a_copy(x, to_x, other).wait_send()
            g1b_copy(y, other, to_y).wait_send()
        g2a_copy(y, to_y).wait_send()
        g2b_copy(x, to_x).wait_send()
        return 0

    lax.fori_loop(1, n, finish_voc, 0)
    lax.fori_loop(1, side, finish_side, 0)
    for bit in range(bits):
        c_copy(bit).wait_send()


def per_device(target_logits, hidden, gain, head_weight, draft_ids, token_ids):
    n = lax.axis_size("voc")
    m = lax.axis_size("tok")
    rows, part = hidden.shape
    vd = target_logits.shape[1]
    width, dv = head_weight.shape
    side = math.isqrt(n)
    half = rows // 2
    cap = 8 * (5 * dv // (16 * n))
    slots = up(cap, 16)
    dp = up(dv, 128)
    chunks = dp // 128
    slot_lanes = up(slots, 128)
    id_rows = n * dv // 128
    bits = m.bit_length() - 1
    vmem = pl.BlockSpec(memory_space=pltpu.VMEM)
    anywhere = pl.BlockSpec(memory_space=pl.ANY)
    dma = pltpu.SemaphoreType.DMA
    d_hidden, loss = pl.pallas_call(
        functools.partial(body, (n, m, vd, dv, cap)),
        out_shape=(
            jax.ShapeDtypeStruct((rows, part), f32),
            jax.ShapeDtypeStruct((1, rows), f32),
        ),
        in_specs=[anywhere] * 6,
        out_specs=(vmem, vmem),
        scratch_shapes=[
            pltpu.VMEM((id_rows, 128), jnp.int32),
            pltpu.VMEM((1, rows), jnp.int32),
            pltpu.VMEM((part // 128, 128), bf16),
            pltpu.VMEM((vd, rows), bf16),
            pltpu.VMEM((dv, width), bf16),
            pltpu.VMEM((n, rows + 16, part), bf16),
            pltpu.VMEM((rows, width), bf16),
            pltpu.VMEM((vd, rows), f32),
            pltpu.VMEM((slots, rows), f32),
            pltpu.VMEM((n, slots, rows), bf16),
            pltpu.VMEM((n, slots, rows), bf16),
            pltpu.VMEM((n * slots, rows), f32),
            pltpu.VMEM((n * chunks, 128), f32),
            pltpu.VMEM((n * chunks, 128), f32),
            pltpu.VMEM((n * chunks, 128), f32),
            pltpu.VMEM((slot_lanes, 128), f32),
            pltpu.VMEM((n, slot_lanes), jnp.int32),
            pltpu.SMEM((n, slot_lanes), jnp.int32),
            pltpu.VMEM((chunks, 128), jnp.int32),
            pltpu.SMEM((chunks, 128), jnp.int32),
            pltpu.VMEM((dv, rows), f32),
            pltpu.VMEM((dv, rows), f32),
            pltpu.VMEM((dp, rows), f32),
            pltpu.VMEM((rows, dp), bf16),
            pltpu.VMEM((side, 16, 128), f32),
            pltpu.VMEM((side, 16, 128), f32),
            pltpu.VMEM((bits, 8, 128), f32),
            pltpu.VMEM((bits, 8, 128), f32),
            pltpu.VMEM((side, side, rows, part), bf16),
            pltpu.VMEM((side, half, part), f32),
            pltpu.VMEM((side, half, part), f32),
            pltpu.VMEM((side, side, half, part), bf16),
            pltpu.VMEM((side, side, half, part), bf16),
            pltpu.VMEM((side, half, part), bf16),
            pltpu.VMEM((side, half, part), bf16),
            pltpu.VMEM((side, half, part), bf16),
            pltpu.VMEM((side, half, part), bf16),
            dma((8,)),
            pltpu.SemaphoreType.REGULAR,
            dma((side,)),
            dma((side,)),
            dma((side, side)),
            dma((side, side)),
            dma((n,)),
            dma((n,)),
            dma((n,)),
            dma((n,)),
            dma((side,)),
            dma((side,)),
            dma((side,)),
            dma((side,)),
            dma((bits,)),
            dma((bits,)),
            dma((side, side)),
            dma((side, side)),
            dma((side, side)),
            dma((side, side)),
            dma((side,)),
            dma((side,)),
            dma((side,)),
            dma((side,)),
        ],
        compiler_params=pltpu.CompilerParams(
            collective_id=0, has_side_effects=True, vmem_limit_bytes=60 * 1024 * 1024
        ),
    )(
        draft_ids.reshape(id_rows, 128),
        token_ids.reshape(1, rows),
        gain.reshape(part // 128, 128),
        hidden,
        target_logits.T,
        head_weight.T,
    )
    return d_hidden, loss.reshape(rows)


def solution(mesh):
    in_specs = (P("tok", "voc"), P("tok", "voc"), P("voc"), P(None, "voc"), P(), P("tok"))
    out_specs = (P("tok", "voc"), P("tok"))
    return jax.shard_map(
        per_device, mesh=mesh, in_specs=in_specs, out_specs=out_specs, check_vma=False
    )
```

time: 85.7 us -> 52.9 us (0.62)
  the two profiles are of different devices: /device:TPU:1 before, /device:TPU:8 now
where the time goes in v2:
time: 52.9 us; the launch traced here: 52.8 us
  Pallas kernels  49.4 us (93%)
  local copies, waits for them, and re-layouts  2.74 us (5%)
  between operations  0.64 us (1%)
    pallas_call x1, Pallas kernels, per_device(): pl.pallas_call(functools.partial(body, (n, m, vd, dv, cap)), out_shape=(j...  49.4 us
    unnamed x2, local copies, waits for them, and re-layouts  2.74 us

profile of v2, /device:TPU:8, one launch (start us, length us, event | category | flops | bytes accessed | tf_op | source)
XLA Modules:
  0.0 52.8 jit_solution(17808565838525288519)
XLA Ops:
  0.6 49.4 %shard_map.77 = (f32[128,256]{1,0:T(8,128)}, f32[1,128]{1,0:T(1,128)}) custom-call(s32[125,128]{1,0:T(8,128)} %bitcast.8, s32[1,128]{1,0:T(1,128)} %bitcast.9, bf16[2,128]{1,0:T(2,128)(2,1)} %bitcast.10, bf16[128,256]{1,0:T(8,128)(2,1)} %hid_hbm.1, bf16[8016,128]{1,0:T(8,128)(2,1)} %bitcast.7, bf16[1000,4096]{1,0:T(8,128)(2,1)} %bitcast.6), custom_call_target="tpu_custom_call" | custom-call | tf_op jit(solution)/shard_map/pallas_call | solution.py:663
  50.0 1.6 %copy.10 = f32[128,256]{1,0:T(8,128)} copy(f32[128,256]{1,0:T(8,128)} %get-tuple-element.8) | data formatting | bytes 262144
  51.6 1.2 %copy.11 = f32[128]{0:T(128)} copy(f32[128]{0:T(128)} %bitcast.11) | data formatting | bytes 1024

commit v3 on v2

--- a/solution.py
+++ b/solution.py
@@ -54,8 +54,10 @@
     grad,
     stat_x,
     stat_y,
-    count_out,
-    count_in,
+    cross_x,
+    cross_y,
+    count,
+    count_all,
     gsend,
     own_a,
     own_b,
@@ -67,6 +69,7 @@
     g2b,
     local_sem,
     entered,
+    greeted,
     ha_first,
     hb_first,
     ha_next,
@@ -79,8 +82,14 @@
     sx_recv,
     sy_send,
     sy_recv,
+    tx_send,
+    tx_recv,
+    ty_send,
+    ty_recv,
     c_send,
     c_recv,
+    t_send,
+    t_recv,
     ga_send,
     gb_send,
     g1a_recv,
@@ -92,7 +101,6 @@
 ):
     n, m, vd, dv, cap = dims
     side = math.isqrt(n)
-    bits = m.bit_length() - 1
     part = hall.shape[2]
     rows = nrm.shape[0]
     half = rows // 2
@@ -109,9 +117,6 @@
 
     def along_y(step):
         return lax.rem(y + step, side)
-
-    def partner(bit):
-        return i + (1 - 2 * lax.rem(i // 2**bit, 2)) * 2**bit
 
     copy_ids = pltpu.make_async_copy(ids_hbm, ids_v, local_sem.at[0])
     copy_hid = pltpu.make_async_copy(hid_hbm, hall.at[j, 0:rows], local_sem.at[1])
@@ -127,15 +132,28 @@
     copy_w.start()
 
     barrier = pltpu.get_barrier_semaphore()
+    hub = j == 0
 
     def greet(step, _):
         for peer in (along_x(step) * side + y, x * side + along_y(step)):
-            pl.semaphore_signal(barrier, inc=1, device_id=(i, peer), device_id_type=MESH)
+
+            @pl.when(peer != 0)
+            def _():
+                pl.semaphore_signal(barrier, inc=1, device_id=(i, peer), device_id_type=MESH)
+
         return 0
 
     lax.fori_loop(1, side, greet, 0)
-    for bit in range(bits):
-        pl.semaphore_signal(barrier, inc=1, device_id=(partner(bit), j), device_id_type=MESH)
+
+    @pl.when(hub)
+    def _():
+        def greet_tok(step, _):
+            peer = lax.rem(i + step, m)
+            pl.semaphore_signal(barrier, inc=1, device_id=(peer, j), device_id_type=MESH)
+            return 0
+
+        lax.fori_loop(1, m, greet_tok, 0)
+
 
     copy_ids.wait()
     lane = lax.broadcasted_iota(jnp.int32, (chunks, 128), 1)
@@ -194,7 +212,17 @@
     wide_gain = jnp.concatenate([wide_gain[r : r + 1, :] for r in range(part // 128)], axis=1)
     hall[j, rows : rows + 16, :] = jnp.broadcast_to(wide_gain, (16, part)).astype(bf16)
 
-    pl.semaphore_wait(barrier, 2 * (side - 1) + bits)
+    @pl.when(j != 0)
+    def _():
+        pl.semaphore_wait(barrier, 2 * (side - 1))
+
+    @pl.when((j != 0) & ((x == 0) | (y == 0)))
+    def _():
+        pl.semaphore_signal(greeted, inc=1, device_id=(i, 0), device_id_type=MESH)
+
+    @pl.when(hub)
+    def _():
+        pl.semaphore_wait(greeted, 2 * (side - 1))
 
     def ha_copy(block, to_x, to_y, send_sem):
         piece = hall.at[block, 0:half]
@@ -251,12 +279,12 @@
         cols = col_v[pl.ds(at, chunks), :]
         found = jnp.zeros((slots, 128), f32)
         for c in range(chunks):
-            found = jnp.where(slot_row == keys[c : c + 1, :], cols[c : c + 1, :], found)
+            found = jnp.where(slot_row == keys[c : c + 1, :], cols[c : c + 1, :] - vd, found)
         return jnp.where(slot_lane == k, jnp.sum(found, axis=1, keepdims=True), acc)
 
     slot_f[...] = jnp.zeros_like(slot_f)
     slot_f[0:slots, :] = lax.fori_loop(0, n, slot_step, jnp.zeros((slots, 128), f32))
-    slot_v[...] = jnp.clip(slot_f[...].T[0:n, :].astype(jnp.int32), 0, vd - 1)
+    slot_v[...] = jnp.clip(slot_f[...].T[0:n, :].astype(jnp.int32) + vd, 0, vd)
     copy_slot = pltpu.make_async_copy(slot_v, slot_s, local_sem.at[6])
     copy_idx = pltpu.make_async_copy(idx_v, idx_s, local_sem.at[7])
     copy_slot.start()
@@ -287,25 +315,36 @@
     valid = lax.fori_loop(0, n, valid_step, jnp.zeros((rows, 128), f32))
     valid = jnp.max(valid.T, axis=0, keepdims=True)
 
-    def c_copy(bit):
-        return pltpu.make_async_remote_copy(
-            src_ref=count_out.at[bit],
-            dst_ref=count_in.at[bit],
-            send_sem=c_send.at[bit],
-            recv_sem=c_recv.at[bit],
-            device_id=(partner(bit), j),
-            device_id_type=MESH,
-        )
-
-    def c_start(bit, value):
-        count_out[bit] = value
-        c_copy(bit).start()
-
-    def c_sum(bit):
-        c_copy(bit).wait_recv()
-        return count_out[bit] + count_in[bit]
-
-    c_start(0, jnp.broadcast_to(jnp.sum(valid, axis=1, keepdims=True), (8, 128)))
+    def c_copy(slot, peer):
+        return pltpu.make_async_remote_copy(
+            src_ref=count.at[i],
+            dst_ref=count.at[slot],
+            send_sem=c_send.at[peer],
+            recv_sem=c_recv.at[slot],
+            device_id=(peer, j),
+            device_id_type=MESH,
+        )
+
+    def t_copy(peer):
+        return pltpu.make_async_remote_copy(
+            src_ref=count_all,
+            dst_ref=count_all,
+            send_sem=t_send.at[peer],
+            recv_sem=t_recv,
+            device_id=(i, peer),
+            device_id_type=MESH,
+        )
+
+    @pl.when(hub)
+    def _():
+        pl.semaphore_wait(barrier, m - 1)
+        count[i] = jnp.broadcast_to(jnp.sum(valid, axis=1, keepdims=True), (8, 128))
+
+        def c_start(step, _):
+            c_copy(i, lax.rem(i + step, m)).start()
+            return 0
+
+        lax.fori_loop(1, m, c_start, 0)
 
     copy_x.wait()
     parts = 3
@@ -322,6 +361,7 @@
     copy_slot.wait()
     copy_idx.wait()
     stage[...] = jnp.zeros_like(stage)
+    table[vd : vd + 8, :] = jnp.full((8, rows), -1e30, f32)
 
     def p_copy(slot, peer):
         return pltpu.make_async_remote_copy(
@@ -338,15 +378,17 @@
             stage[at : at + 1, :] = table[pl.ds(slot_s[k, at], 1), :]
         return stage[...].astype(bf16)
 
-    def pick_step(step, _):
+    def pick_mass():
+        return jnp.sum(jnp.exp(stage[0:cap, :] - top_target), axis=0, keepdims=True)
+
+    def pick_step(step, acc):
         peer = lax.rem(j + step, n)
         psend[peer] = pick(peer)
-        p_copy(j, peer).start()
-        return 0
-
-    pl.semaphore_wait(entered, side - 1)
-    lax.fori_loop(1, n, pick_step, 0)
+        return acc + pick_mass()
+
+    mass_here = lax.fori_loop(1, n, pick_step, jnp.zeros((1, rows), f32))
     precv[j] = pick(j)
+    mass_here += pick_mass()
 
     total_target = lax.fori_loop(
         0,
@@ -359,8 +401,6 @@
         ),
         jnp.zeros((1, rows), f32),
     )
-    if bits > 1:
-        c_start(1, c_sum(0))
 
     def h_rest(step, _):
         from_y = along_y(step)
@@ -380,6 +420,13 @@
         return 0
 
     lax.fori_loop(1, side, h_rest, 0)
+
+    def p_start(step, _):
+        p_copy(j, lax.rem(j + step, n)).start()
+        return 0
+
+    pl.semaphore_wait(entered, side - 1)
+    lax.fori_loop(1, n, p_start, 0)
 
     def square(k, acc):
         wide = hall[k, 0:rows, :].astype(f32)
@@ -397,8 +444,6 @@
 
     lax.fori_loop(0, n, normalise, 0)
     inv_row = jnp.broadcast_to(inv, (rows, 128)).T[0:1, :]
-    if bits > 2:
-        c_start(2, c_sum(1))
 
     copy_w.wait()
     lt[...] = lax.dot_general(w_v[...], nrm[...], NT, preferred_element_type=f32)
@@ -407,34 +452,28 @@
     lifted = jnp.exp(draft - top_draft)
     total_draft = jnp.sum(lifted, axis=0, keepdims=True)
     cross_draft = jnp.sum(lifted * draft, axis=0, keepdims=True)
-    if bits > 3:
-        c_start(3, c_sum(2))
-
-    def p_wait(step, _):
-        p_copy(lax.rem(j + step, n), j).wait_recv()
-        return 0
-
-    lax.fori_loop(1, n, p_wait, 0)
-
-    def widen(k, _):
-        pwide[pl.ds(pl.multiple_of(k * slots, 8), slots), :] = precv[k].astype(f32)
-        return 0
-
-    lax.fori_loop(0, n, widen, 0)
-    for at in range(dv):
-        pt[at : at + 1, :] = pwide[pl.ds(idx_s[at // 128, at % 128], 1), :]
-    picked = pt[...]
-    top_picked = jnp.max(picked, axis=0, keepdims=True)
-    raised = jnp.exp(picked - top_picked)
-    total_picked = jnp.sum(raised, axis=0, keepdims=True)
-    cross_picked = jnp.sum(raised * lt[...], axis=0, keepdims=True)
-
-    tops = (top_target, top_picked, top_picked, top_draft, top_draft)
-    sums = (total_target, total_picked, cross_picked, total_draft, cross_draft)
+
+    tops = (top_target, top_target, top_draft, top_draft)
+    sums = (total_target, mass_here, total_draft, cross_draft)
     stat_x[x] = jnp.zeros((16, 128), f32)
-    for r in range(5):
+    for r in range(4):
         stat_x[x, r : r + 1, :] = tops[r]
         stat_x[x, 8 + r : 9 + r, :] = sums[r]
+
+    @pl.when(hub)
+    def _():
+        def c_wait(step, _):
+            c_copy(lax.rem(i + step, m), i).wait_recv()
+            return 0
+
+        lax.fori_loop(1, m, c_wait, 0)
+        count_all[...] = jnp.sum(count[...], axis=0)
+
+        def t_start(peer, _):
+            t_copy(peer).start()
+            return 0
+
+        lax.fori_loop(1, n, t_start, 0)
 
     def sx_copy(slot, to_x):
         return pltpu.make_async_remote_copy(
@@ -467,8 +506,6 @@
 
     for step in range(1, side):
         sx_copy(x, along_x(step)).start()
-    valid_total = c_sum(bits - 1)[0:1, :]
-    weight = valid * (float(rows * m) / valid_total)
     for step in range(1, side):
         sx_copy(along_x(step), x).wait_recv()
     top, total = merge(stat_x)
@@ -481,20 +518,57 @@
     top, total = merge(stat_y)
 
     target_lse = top[0:1, :] + jnp.log(total[0:1, :])
-    factor = jnp.exp(top[1:2, :] - target_lse)
-    mass = total[1:2, :] * factor
-    cross = total[2:3, :] * factor
-    draft_lse = top[3:4, :] + jnp.log(total[3:4, :])
-    loss_ref[...] = weight * (mass * draft_lse - cross)
-    spread = weight * (mass * (total[4:5, :] / total[3:4, :]) - cross)
-    shrink = inv_row * inv_row * spread / width
-
-    soft = jnp.exp(lt[...] - draft_lse)
+    mass = total[1:2, :] * jnp.exp(top[1:2, :] - target_lse)
+    draft_lse = top[2:3, :] + jnp.log(total[2:3, :])
+    mean_draft = total[3:4, :] / total[2:3, :]
+    wide_grad[dv:, :] = jnp.zeros((wide_grad.shape[0] - dv, rows), f32)
+    wide_grad[0:dv, :] = mass * jnp.exp(lt[...] - draft_lse)
+
+    def p_wait(step, _):
+        p_copy(lax.rem(j + step, n), j).wait_recv()
+        return 0
+
+    lax.fori_loop(1, n, p_wait, 0)
+
+    def widen(k, _):
+        pwide[pl.ds(pl.multiple_of(k * slots, 8), slots), :] = precv[k].astype(f32)
+        return 0
+
+    lax.fori_loop(0, n, widen, 0)
+    for at in range(dv):
+        pt[at : at + 1, :] = pwide[pl.ds(idx_s[at // 128, at % 128], 1), :]
+    @pl.when(j != 0)
+    def _():
+        t_copy(0).wait_recv()
+
+    weight = valid * (float(rows * m) / count_all[0:1, :])
     probs = jnp.exp(pt[...] - target_lse)
-    wide_grad[dv:, :] = jnp.zeros((wide_grad.shape[0] - dv, rows), f32)
-    wide_grad[0:dv, :] = weight * (mass * soft - probs)
+    wide_grad[0:dv, :] = weight * (wide_grad[0:dv, :] - probs)
     grad[...] = wide_grad[...].T.astype(bf16)
-    shrink = jnp.broadcast_to(shrink, (rows, rows)).T[:, 0:1]
+    cross_x[x] = jnp.broadcast_to(jnp.sum(probs * lt[...], axis=0, keepdims=True), (8, rows))
+
+    def tx_copy(slot, to_x):
+        return pltpu.make_async_remote_copy(
+            src_ref=cross_x.at[slot],
+            dst_ref=cross_x.at[slot],
+            send_sem=tx_send.at[to_x],
+            recv_sem=tx_recv.at[slot],
+            device_id=(i, to_x * side + y),
+            device_id_type=MESH,
+        )
+
+    def ty_copy(slot, to_y):
+        return pltpu.make_async_remote_copy(
+            src_ref=cross_y.at[slot],
+            dst_ref=cross_y.at[slot],
+            send_sem=ty_send.at[to_y],
+            recv_sem=ty_recv.at[slot],
+            device_id=(i, x * side + to_y),
+            device_id_type=MESH,
+        )
+
+    for step in range(1, side):
+        tx_copy(x, along_x(step)).start()
 
     def term(to_x, to_y):
         at = pl.multiple_of((to_x * side + to_y) * part, part)
@@ -550,6 +624,12 @@
     value = term(x, y)
     own_a[y] = value[0:half, :]
     own_b[x] = value[half:rows, :]
+
+    for step in range(1, side):
+        tx_copy(along_x(step), x).wait_recv()
+    cross_y[y] = jnp.sum(cross_x[...], axis=0)
+    for step in range(1, side):
+        ty_copy(y, along_y(step)).start()
 
     def sum_a(to_y):
         acc = own_a[to_y]
@@ -597,6 +677,13 @@
         return 0
 
     lax.fori_loop(1, side, g_second, 0)
+    for step in range(1, side):
+        ty_copy(along_y(step), y).wait_recv()
+    cross = jnp.sum(cross_y[...], axis=0)[0:1, :]
+    loss_ref[...] = weight * (mass * draft_lse - cross)
+    spread = weight * (mass * mean_draft - cross)
+    shrink = inv_row * inv_row * spread / width
+    shrink = jnp.broadcast_to(shrink, (rows, rows)).T[:, 0:1]
     first = sum_a(y)
     second = sum_b(x)
     for step in range(1, side):
@@ -629,6 +716,8 @@
             hb_forward(origin, step).wait_send()
         sx_copy(x, to_x).wait_send()
         sy_copy(y, to_y).wait_send()
+        tx_copy(x, to_x).wait_send()
+        ty_copy(y, to_y).wait_send()
         for other in range(side):
             g1a_copy(x, to_x, other).wait_send()
             g1b_copy(y, other, to_y).wait_send()
@@ -638,8 +727,19 @@
 
     lax.fori_loop(1, n, finish_voc, 0)
     lax.fori_loop(1, side, finish_side, 0)
-    for bit in range(bits):
-        c_copy(bit).wait_send()
+
+    @pl.when(hub)
+    def _():
+        def finish_tok(step, _):
+            c_copy(i, lax.rem(i + step, m)).wait_send()
+            return 0
+
+        def finish_total(peer, _):
+            t_copy(peer).wait_send()
+            return 0
+
+        lax.fori_loop(1, m, finish_tok, 0)
+        lax.fori_loop(1, n, finish_total, 0)
 
 
 def per_device(target_logits, hidden, gain, head_weight, draft_ids, token_ids):
@@ -656,7 +756,6 @@
     chunks = dp // 128
     slot_lanes = up(slots, 128)
     id_rows = n * dv // 128
-    bits = m.bit_length() - 1
     vmem = pl.BlockSpec(memory_space=pltpu.VMEM)
     anywhere = pl.BlockSpec(memory_space=pl.ANY)
     dma = pltpu.SemaphoreType.DMA
@@ -676,7 +775,7 @@
             pltpu.VMEM((dv, width), bf16),
             pltpu.VMEM((n, rows + 16, part), bf16),
             pltpu.VMEM((rows, width), bf16),
-            pltpu.VMEM((vd, rows), f32),
+            pltpu.VMEM((vd + 8, rows), f32),
             pltpu.VMEM((slots, rows), f32),
             pltpu.VMEM((n, slots, rows), bf16),
             pltpu.VMEM((n, slots, rows), bf16),
@@ -695,8 +794,10 @@
             pltpu.VMEM((rows, dp), bf16),
             pltpu.VMEM((side, 16, 128), f32),
             pltpu.VMEM((side, 16, 128), f32),
-            pltpu.VMEM((bits, 8, 128), f32),
-            pltpu.VMEM((bits, 8, 128), f32),
+            pltpu.VMEM((side, 8, 128), f32),
+            pltpu.VMEM((side, 8, 128), f32),
+            pltpu.VMEM((m, 8, 128), f32),
+            pltpu.VMEM((8, 128), f32),
             pltpu.VMEM((side, side, rows, part), bf16),
             pltpu.VMEM((side, half, part), f32),
             pltpu.VMEM((side, half, part), f32),
@@ -708,6 +809,7 @@
             pltpu.VMEM((side, half, part), bf16),
             dma((8,)),
             pltpu.SemaphoreType.REGULAR,
+            pltpu.SemaphoreType.REGULAR,
             dma((side,)),
             dma((side,)),
             dma((side, side)),
@@ -720,8 +822,14 @@
             dma((side,)),
             dma((side,)),
             dma((side,)),
-            dma((bits,)),
-            dma((bits,)),
+            dma((side,)),
+            dma((side,)),
+            dma((side,)),
+            dma((side,)),
+            dma((m,)),
+            dma((m,)),
+            dma((n,)),
+            dma,
             dma((side, side)),
             dma((side, side)),
             dma((side, side)),

time: 52.9 us -> 47.7 us (0.902)
  the two profiles are of different devices: /device:TPU:8 before, /device:TPU:64 now
where the time goes in v3:
time: 47.7 us; the launch traced here: 47.5 us
  Pallas kernels  44.2 us (93%)
  local copies, waits for them, and re-layouts  2.74 us (6%)
  between operations  0.64 us (1%)
    pallas_call x1, Pallas kernels, per_device(): pl.pallas_call(functools.partial(body, (n, m, vd, dv, cap)), out_shape=(j...  44.2 us
    unnamed x2, local copies, waits for them, and re-layouts  2.74 us

profile of v3, /device:TPU:64, one launch (start us, length us, event | category | flops | bytes accessed | tf_op | source)
XLA Modules:
  0.0 47.5 jit_solution(2616322534501928866)
XLA Ops:
  0.6 44.2 %shard_map.77 = (f32[128,256]{1,0:T(8,128)}, f32[1,128]{1,0:T(1,128)}) custom-call(s32[125,128]{1,0:T(8,128)} %bitcast.8, s32[1,128]{1,0:T(1,128)} %bitcast.9, bf16[2,128]{1,0:T(2,128)(2,1)} %bitcast.10, bf16[128,256]{1,0:T(8,128)(2,1)} %hid_hbm.1, bf16[8016,128]{1,0:T(8,128)(2,1)} %bitcast.7, bf16[1000,4096]{1,0:T(8,128)(2,1)} %bitcast.6), custom_call_target="tpu_custom_call" | custom-call | tf_op jit(solution)/shard_map/pallas_call | solution.py:762
  44.8 1.6 %copy.10 = f32[128,256]{1,0:T(8,128)} copy(f32[128,256]{1,0:T(8,128)} %get-tuple-element.8) | data formatting | bytes 262144
  46.4 1.2 %copy.11 = f32[128]{0:T(128)} copy(f32[128]{0:T(128)} %bitcast.11) | data formatting | bytes 1024

commit v4 on v3

--- a/solution.py
+++ b/solution.py
@@ -52,10 +52,11 @@
     pt,
     wide_grad,
     grad,
-    stat_x,
-    stat_y,
+    stats,
     cross_x,
     cross_y,
+    square_x,
+    square_y,
     count,
     count_all,
     gsend,
@@ -78,10 +79,12 @@
     hb_recv,
     p_send,
     p_recv,
-    sx_send,
-    sx_recv,
-    sy_send,
-    sy_recv,
+    s_send,
+    s_recv,
+    qx_send,
+    qx_recv,
+    qy_send,
+    qy_recv,
     tx_send,
     tx_recv,
     ty_send,
@@ -210,7 +213,6 @@
     copy_gain.wait()
     wide_gain = gain_v[...].astype(f32)
     wide_gain = jnp.concatenate([wide_gain[r : r + 1, :] for r in range(part // 128)], axis=1)
-    hall[j, rows : rows + 16, :] = jnp.broadcast_to(wide_gain, (16, part)).astype(bf16)
 
     @pl.when(j != 0)
     def _():
@@ -236,7 +238,7 @@
         )
 
     def hb_copy(block, to_x, to_y, send_sem):
-        piece = hall.at[block, half : rows + 16]
+        piece = hall.at[block, half:rows]
         return pltpu.make_async_remote_copy(
             src_ref=piece,
             dst_ref=piece,
@@ -269,6 +271,34 @@
 
     lax.fori_loop(1, side, h_first, 0)
     lax.fori_loop(1, side, h_own, 0)
+
+    own_hidden = hall[j, 0:rows, :].astype(f32)
+    own_squares = jnp.sum(own_hidden * own_hidden, axis=1, keepdims=True)
+    square_x[x] = jnp.broadcast_to(own_squares, (rows, 128)).T[0:8, :]
+    square_x[x, 1 : 1 + part // 128, :] = gain_v[...].astype(f32)
+
+    def qx_copy(slot, to_x):
+        return pltpu.make_async_remote_copy(
+            src_ref=square_x.at[slot],
+            dst_ref=square_x.at[slot],
+            send_sem=qx_send.at[to_x],
+            recv_sem=qx_recv.at[slot],
+            device_id=(i, to_x * side + y),
+            device_id_type=MESH,
+        )
+
+    def qy_copy(slot, to_y):
+        return pltpu.make_async_remote_copy(
+            src_ref=square_y.at[slot],
+            dst_ref=square_y.at[slot],
+            send_sem=qy_send.at[to_y],
+            recv_sem=qy_recv.at[slot],
+            device_id=(i, x * side + to_y),
+            device_id_type=MESH,
+        )
+
+    for step in range(1, side):
+        qx_copy(x, along_x(step)).start()
 
     slot_row = lax.broadcasted_iota(jnp.int32, (slots, 128), 0).astype(f32)
     slot_lane = lax.broadcasted_iota(jnp.int32, (slots, 128), 1)
@@ -302,6 +332,11 @@
         return 0
 
     lax.fori_loop(1, side, h_pass, 0)
+    for step in range(1, side):
+        qx_copy(along_x(step), x).wait_recv()
+    square_y[y] = square_x[...]
+    for step in range(1, side):
+        qy_copy(y, along_y(step)).start()
 
     copy_tok.wait()
     token_rows = jnp.broadcast_to(tok_v[...].astype(f32), (rows, rows)).T
@@ -402,51 +437,46 @@
         jnp.zeros((1, rows), f32),
     )
 
-    def h_rest(step, _):
-        from_y = along_y(step)
-
-        def h_rest_a(xs, _):
-            ha_copy(xs * side + from_y, x, from_y, ha_next.at[0, 0]).wait_recv()
-            return 0
-
-        lax.fori_loop(0, side, h_rest_a, 0)
-        from_x = along_x(step)
-
-        def h_rest_b(ys, _):
-            hb_copy(from_x * side + ys, from_x, y, hb_next.at[0, 0]).wait_recv()
-            return 0
-
-        lax.fori_loop(0, side, h_rest_b, 0)
-        return 0
-
-    lax.fori_loop(1, side, h_rest, 0)
+    for step in range(1, side):
+        qy_copy(along_y(step), y).wait_recv()
+    squares = jnp.sum(jnp.sum(square_y[...], axis=0), axis=0)[0:1, :]
+    inv_row = lax.rsqrt(squares / width + epsilon)
+    inv = jnp.broadcast_to(inv_row, (rows, rows)).T[:, 0:1]
 
     def p_start(step, _):
         p_copy(j, lax.rem(j + step, n)).start()
         return 0
 
-    pl.semaphore_wait(entered, side - 1)
-    lax.fori_loop(1, n, p_start, 0)
-
-    def square(k, acc):
+    def normalise(xs, ys):
+        k = xs * side + ys
         wide = hall[k, 0:rows, :].astype(f32)
-        return acc + wide * wide
-
-    squares = lax.fori_loop(0, n, square, jnp.zeros((rows, part), f32))
-    inv = lax.rsqrt(jnp.sum(squares, axis=1, keepdims=True) / width + epsilon)
-
-    def normalise(k, _):
-        wide = hall[k, 0:rows, :].astype(f32)
-        gains = hall[k, rows : rows + 16, :].astype(f32)[0:1, :]
+        tile = square_y[ys, xs]
+        gains = jnp.concatenate([tile[r + 1 : r + 2, :] for r in range(part // 128)], axis=1)
         at = pl.multiple_of(k * part, part)
         nrm[:, pl.ds(at, part)] = (wide * inv * gains).astype(bf16)
-        return 0
-
-    lax.fori_loop(0, n, normalise, 0)
-    inv_row = jnp.broadcast_to(inv, (rows, 128)).T[0:1, :]
-
-    copy_w.wait()
-    lt[...] = lax.dot_general(w_v[...], nrm[...], NT, preferred_element_type=f32)
+
+    for step in range(side):
+        from_x = along_x(step)
+        for other in range(1, side):
+            from_y = along_y(other)
+            ha_copy(from_x * side + from_y, x, from_y, ha_next.at[0, 0]).wait_recv()
+        if step:
+            for other in range(side):
+                hb_copy(from_x * side + other, from_x, y, hb_next.at[0, 0]).wait_recv()
+        if step == 0:
+            pl.semaphore_wait(entered, side - 1)
+            lax.fori_loop(1, n, p_start, 0)
+        for other in range(side):
+            normalise(from_x, other)
+        if step == 0:
+            copy_w.wait()
+        at = pl.ds(pl.multiple_of(from_x * side * part, part), side * part)
+        share = lax.dot_general(w_v[:, at], nrm[:, at], NT, preferred_element_type=f32)
+        if step:
+            lt[...] += share
+        else:
+            lt[...] = share
+
     draft = lt[...]
     top_draft = jnp.max(draft, axis=0, keepdims=True)
     lifted = jnp.exp(draft - top_draft)
@@ -455,10 +485,10 @@
 
     tops = (top_target, top_target, top_draft, top_draft)
     sums = (total_target, mass_here, total_draft, cross_draft)
-    stat_x[x] = jnp.zeros((16, 128), f32)
+    stats[j] = jnp.zeros((16, 128), f32)
     for r in range(4):
-        stat_x[x, r : r + 1, :] = tops[r]
-        stat_x[x, 8 + r : 9 + r, :] = sums[r]
+        stats[j, r : r + 1, :] = tops[r]
+        stats[j, 8 + r : 9 + r, :] = sums[r]
 
     @pl.when(hub)
     def _():
@@ -475,47 +505,36 @@
 
         lax.fori_loop(1, n, t_start, 0)
 
-    def sx_copy(slot, to_x):
-        return pltpu.make_async_remote_copy(
-            src_ref=stat_x.at[slot],
-            dst_ref=stat_x.at[slot],
-            send_sem=sx_send.at[to_x],
-            recv_sem=sx_recv.at[slot],
-            device_id=(i, to_x * side + y),
-            device_id_type=MESH,
-        )
-
-    def sy_copy(slot, to_y):
-        return pltpu.make_async_remote_copy(
-            src_ref=stat_y.at[slot],
-            dst_ref=stat_y.at[slot],
-            send_sem=sy_send.at[to_y],
-            recv_sem=sy_recv.at[slot],
-            device_id=(i, x * side + to_y),
+    def s_copy(slot, peer):
+        return pltpu.make_async_remote_copy(
+            src_ref=stats.at[slot],
+            dst_ref=stats.at[slot],
+            send_sem=s_send.at[peer],
+            recv_sem=s_recv.at[slot],
+            device_id=(i, peer),
             device_id_type=MESH,
         )
 
     def merge(ref):
         top = ref[0, 0:8, :]
-        for k in range(1, side):
+        for k in range(1, n):
             top = jnp.maximum(top, ref[k, 0:8, :])
         total = jnp.zeros((8, 128), f32)
-        for k in range(side):
+        for k in range(n):
             total += ref[k, 8:16, :] * jnp.exp(ref[k, 0:8, :] - top)
         return top, total
 
-    for step in range(1, side):
-        sx_copy(x, along_x(step)).start()
-    for step in range(1, side):
-        sx_copy(along_x(step), x).wait_recv()
-    top, total = merge(stat_x)
-    stat_y[y, 0:8, :] = top
-    stat_y[y, 8:16, :] = total
-    for step in range(1, side):
-        sy_copy(y, along_y(step)).start()
-    for step in range(1, side):
-        sy_copy(along_y(step), y).wait_recv()
-    top, total = merge(stat_y)
+    def s_start(step, _):
+        s_copy(j, lax.rem(j + step, n)).start()
+        return 0
+
+    def s_wait(step, _):
+        s_copy(lax.rem(j + step, n), j).wait_recv()
+        return 0
+
+    lax.fori_loop(1, n, s_start, 0)
+    lax.fori_loop(1, n, s_wait, 0)
+    top, total = merge(stats)
 
     target_lse = top[0:1, :] + jnp.log(total[0:1, :])
     mass = total[1:2, :] * jnp.exp(top[1:2, :] - target_lse)
@@ -524,17 +543,17 @@
     wide_grad[dv:, :] = jnp.zeros((wide_grad.shape[0] - dv, rows), f32)
     wide_grad[0:dv, :] = mass * jnp.exp(lt[...] - draft_lse)
 
+    def widen(k):
+        pwide[pl.ds(pl.multiple_of(k * slots, 8), slots), :] = precv[k].astype(f32)
+
     def p_wait(step, _):
-        p_copy(lax.rem(j + step, n), j).wait_recv()
-        return 0
-
+        slot = lax.rem(j + step, n)
+        p_copy(slot, j).wait_recv()
+        widen(slot)
+        return 0
+
+    widen(j)
     lax.fori_loop(1, n, p_wait, 0)
-
-    def widen(k, _):
-        pwide[pl.ds(pl.multiple_of(k * slots, 8), slots), :] = precv[k].astype(f32)
-        return 0
-
-    lax.fori_loop(0, n, widen, 0)
     for at in range(dv):
         pt[at : at + 1, :] = pwide[pl.ds(idx_s[at // 128, at % 128], 1), :]
     @pl.when(j != 0)
@@ -704,6 +723,7 @@
     def finish_voc(step, _):
         peer = lax.rem(j + step, n)
         p_copy(j, peer).wait_send()
+        s_copy(j, peer).wait_send()
         return 0
 
     def finish_side(step, _):
@@ -714,8 +734,8 @@
         for origin in range(side):
             ha_forward(origin, step).wait_send()
             hb_forward(origin, step).wait_send()
-        sx_copy(x, to_x).wait_send()
-        sy_copy(y, to_y).wait_send()
+        qx_copy(x, to_x).wait_send()
+        qy_copy(y, to_y).wait_send()
         tx_copy(x, to_x).wait_send()
         ty_copy(y, to_y).wait_send()
         for other in range(side):
@@ -773,7 +793,7 @@
             pltpu.VMEM((part // 128, 128), bf16),
             pltpu.VMEM((vd, rows), bf16),
             pltpu.VMEM((dv, width), bf16),
-            pltpu.VMEM((n, rows + 16, part), bf16),
+            pltpu.VMEM((n, rows, part), bf16),
             pltpu.VMEM((rows, width), bf16),
             pltpu.VMEM((vd + 8, rows), f32),
             pltpu.VMEM((slots, rows), f32),
@@ -792,10 +812,11 @@
             pltpu.VMEM((dv, rows), f32),
             pltpu.VMEM((dp, rows), f32),
             pltpu.VMEM((rows, dp), bf16),
-            pltpu.VMEM((side, 16, 128), f32),
-            pltpu.VMEM((side, 16, 128), f32),
+            pltpu.VMEM((n, 16, 128), f32),
             pltpu.VMEM((side, 8, 128), f32),
             pltpu.VMEM((side, 8, 128), f32),
+            pltpu.VMEM((side, 8, 128), f32),
+            pltpu.VMEM((side, side, 8, 128), f32),
             pltpu.VMEM((m, 8, 128), f32),
             pltpu.VMEM((8, 128), f32),
             pltpu.VMEM((side, side, rows, part), bf16),
@@ -818,6 +839,8 @@
             dma((n,)),
             dma((n,)),
             dma((n,)),
+            dma((n,)),
+            dma((n,)),
             dma((side,)),
             dma((side,)),
             dma((side,)),

time: 47.7 us -> 46.1 us (0.966)
  Pallas kernels: 44.2 us -> 42.6 us
    pallas_call x1, Pallas kernels: 44.2 us -> 42.6 us  [per_device(): pl.pallas_call(functools.partial(body, (n, m, vd, dv, cap)), out_shape=(j...]
where the time goes in v4:
time: 46.1 us; the launch traced here: 46 us
  Pallas kernels  42.6 us (92%)
  local copies, waits for them, and re-layouts  2.74 us (6%)
  between operations  0.64 us (1%)
    pallas_call x1, Pallas kernels, per_device(): pl.pallas_call(functools.partial(body, (n, m, vd, dv, cap)), out_shape=(j...  42.6 us
    unnamed x2, local copies, waits for them, and re-layouts  2.74 us

profile of v4, /device:TPU:64, one launch (start us, length us, event | category | flops | bytes accessed | tf_op | source)
XLA Modules:
  0.0 46.0 jit_solution(16118835480284949762)
XLA Ops:
  0.6 42.6 %shard_map.77 = (f32[128,256]{1,0:T(8,128)}, f32[1,128]{1,0:T(1,128)}) custom-call(s32[125,128]{1,0:T(8,128)} %bitcast.8, s32[1,128]{1,0:T(1,128)} %bitcast.9, bf16[2,128]{1,0:T(2,128)(2,1)} %bitcast.10, bf16[128,256]{1,0:T(8,128)(2,1)} %hid_hbm.1, bf16[8016,128]{1,0:T(8,128)(2,1)} %bitcast.7, bf16[1000,4096]{1,0:T(8,128)(2,1)} %bitcast.6), custom_call_target="tpu_custom_call" | custom-call | tf_op jit(solution)/shard_map/pallas_call | solution.py:782
  43.2 1.6 %copy.10 = f32[128,256]{1,0:T(8,128)} copy(f32[128,256]{1,0:T(8,128)} %get-tuple-element.8) | data formatting | bytes 262144
  44.8 1.2 %copy.11 = f32[128]{0:T(128)} copy(f32[128]{0:T(128)} %bitcast.11) | data formatting | bytes 1024

commit v5 on v4

--- a/solution.py
+++ b/solution.py
@@ -564,30 +564,6 @@
     probs = jnp.exp(pt[...] - target_lse)
     wide_grad[0:dv, :] = weight * (wide_grad[0:dv, :] - probs)
     grad[...] = wide_grad[...].T.astype(bf16)
-    cross_x[x] = jnp.broadcast_to(jnp.sum(probs * lt[...], axis=0, keepdims=True), (8, rows))
-
-    def tx_copy(slot, to_x):
-        return pltpu.make_async_remote_copy(
-            src_ref=cross_x.at[slot],
-            dst_ref=cross_x.at[slot],
-            send_sem=tx_send.at[to_x],
-            recv_sem=tx_recv.at[slot],
-            device_id=(i, to_x * side + y),
-            device_id_type=MESH,
-        )
-
-    def ty_copy(slot, to_y):
-        return pltpu.make_async_remote_copy(
-            src_ref=cross_y.at[slot],
-            dst_ref=cross_y.at[slot],
-            send_sem=ty_send.at[to_y],
-            recv_sem=ty_recv.at[slot],
-            device_id=(i, x * side + to_y),
-            device_id_type=MESH,
-        )
-
-    for step in range(1, side):
-        tx_copy(x, along_x(step)).start()
 
     def term(to_x, to_y):
         at = pl.multiple_of((to_x * side + to_y) * part, part)
@@ -638,6 +614,31 @@
         return 0
 
     lax.fori_loop(0, (side - 1) * (side - 1), g_both, 0)
+    cross_x[x] = jnp.broadcast_to(jnp.sum(jnp.exp(pt[...] - target_lse) * lt[...], axis=0, keepdims=True), (8, rows))
+
+    def tx_copy(slot, to_x):
+        return pltpu.make_async_remote_copy(
+            src_ref=cross_x.at[slot],
+            dst_ref=cross_x.at[slot],
+            send_sem=tx_send.at[to_x],
+            recv_sem=tx_recv.at[slot],
+            device_id=(i, to_x * side + y),
+            device_id_type=MESH,
+        )
+
+    def ty_copy(slot, to_y):
+        return pltpu.make_async_remote_copy(
+            src_ref=cross_y.at[slot],
+            dst_ref=cross_y.at[slot],
+            send_sem=ty_send.at[to_y],
+            recv_sem=ty_recv.at[slot],
+            device_id=(i, x * side + to_y),
+            device_id_type=MESH,
+        )
+
+    for step in range(1, side):
+        tx_copy(x, along_x(step)).start()
+
     lax.fori_loop(1, side, g_column, 0)
     lax.fori_loop(1, side, g_row, 0)
     value = term(x, y)

time: 46.1 us -> 47.4 us (1.028)
  Pallas kernels: 42.6 us -> 43.8 us
    pallas_call x1, Pallas kernels: 42.6 us -> 43.8 us  [per_device(): pl.pallas_call(functools.partial(body, (n, m, vd, dv, cap)), out_shape=(j...]
where the time goes in v5:
time: 47.4 us; the launch traced here: 47.2 us
  Pallas kernels  43.8 us (92%)
  local copies, waits for them, and re-layouts  2.74 us (6%)
  between operations  0.64 us (1%)
    pallas_call x1, Pallas kernels, per_device(): pl.pallas_call(functools.partial(body, (n, m, vd, dv, cap)), out_shape=(j...  43.8 us
    unnamed x2, local copies, waits for them, and re-layouts  2.74 us

profile of v5, /device:TPU:64, one launch (start us, length us, event | category | flops | bytes accessed | tf_op | source)
XLA Modules:
  0.0 47.2 jit_solution(83461603618056525)
XLA Ops:
  0.6 43.8 %shard_map.77 = (f32[128,256]{1,0:T(8,128)}, f32[1,128]{1,0:T(1,128)}) custom-call(s32[125,128]{1,0:T(8,128)} %bitcast.8, s32[1,128]{1,0:T(1,128)} %bitcast.9, bf16[2,128]{1,0:T(2,128)(2,1)} %bitcast.10, bf16[128,256]{1,0:T(8,128)(2,1)} %hid_hbm.1, bf16[8016,128]{1,0:T(8,128)(2,1)} %bitcast.7, bf16[1000,4096]{1,0:T(8,128)(2,1)} %bitcast.6), custom_call_target="tpu_custom_call" | custom-call | tf_op jit(solution)/shard_map/pallas_call | solution.py:783
  44.5 1.6 %copy.10 = f32[128,256]{1,0:T(8,128)} copy(f32[128,256]{1,0:T(8,128)} %get-tuple-element.8) | data formatting | bytes 262144
  46.1 1.2 %copy.11 = f32[128]{0:T(128)} copy(f32[128]{0:T(128)} %bitcast.11) | data formatting | bytes 1024
